TPU v7x, 128 devices: a whole 4x4x4 slice. The times are simulated.
128 devices in a mesh: row: 8 (over x, core), col: 16 (over y, z).
Axes of the slice: x: 4, y: 4, z: 4, core: 2. Of those that a mesh axis runs over, the one named last changes fastest.
Arguments:
- leaf_source: float32 [2, 128, 1024, 256], P(None, ('row', 'col')), may hold values from -6 to 6
- leaf_inv: float32 [128, 2, 512, 512], P(('row', 'col')), as said below
- leaf_low: float32 [128, 2, 512, 512], P(('row', 'col')), may hold values from -0.1875 to 0.1875
- child_count: int32 [128], replicated, may hold values from 256 to 512
- child_owner: int32 [128, 512, 1], replicated, may hold values from 0 to 127; in each aligned block of 512 rows (0 to 511, 512 to 1023, ..., all dimensions but the last counted through in order) at most 6 rows name the same one
- child_slot: int32 [128, 512], replicated, may hold values from 0 to 127
- parent_source: float32 [2, 16384, 256], P(None, ('row', 'col')), may hold values from -6 to 6
- parent_inv: float32 [2, 16384, 16384], P(None, 'row', 'col'), as said below
- kernel_coef: float32 [3, 16384], P(None, ('row', 'col')), may hold values from 0.5 to 2
- p_speed: float32 [16384], P(('row', 'col')), may hold values from 1 to 2
- s_speed: float32 [16384], P(('row', 'col')), may hold values from 0.4 to 0.8
- density: float32 [16384], P(('row', 'col')), may hold values from 0.8 to 1.2
Outputs:
- gradient: float32 [3, 16384], P(None, ('row', 'col'))
Inputs may be any that keep to these rules, and one draw needn't show every extreme that they name: `child_owner`: in each aligned block of 512 rows (one child's rows) no owner appears more than 6 times, and some owner appears exactly 6 times. `leaf_inv`: each child's matrix is unit lower triangular: real part 1 and imaginary part 0 on the diagonal, zero above. `parent_inv`: lower triangular in elimination order: stored row p maps to elimination row ((l div 64) * 8 + r) * 64 + l mod 64 with r = p div (2048), l = p mod (2048); stored columns likewise with 16; the diagonal is 1 (real), entries above it zero.
All inputs are finite; a program needn't handle non-finite values.
Results may differ from a plain program's by a relative error of at most 0.00029.
Values sent between devices are 32-bit elements; how exact they have to be, the bound alone decides.
No kernel may reach another device: no remote copies, remote signals or barrier semaphores. Data moves between devices by JAX's collectives and lax.ppermute only.
A program may use at most 128 MiB of HBM per device.

v0:
```python
import functools

import jax
import jax.numpy as jnp
from jax import lax
from jax.experimental import pallas as pl
from jax.experimental.pallas import tpu as pltpu
from jax.sharding import PartitionSpec as P

SOURCES = 128
CAPACITY = 6
LANES = 128
RING = 4
BATCHES = ((2, 0), (1, 3))
F32 = jnp.float32
BF16 = jnp.bfloat16


def halves(value):
    high = value.astype(BF16)
    return high, (value - high.astype(F32)).astype(BF16)


def dot(left, right, dims=((1,), (0,))):
    return lax.dot_general(left, right, (dims, ((), ())), preferred_element_type=F32)


def left_parts(real_part, imag_part):
    real_high, real_low = halves(real_part)
    imag_high, imag_low = halves(imag_part)
    return jnp.concatenate([real_high, imag_high, real_high, imag_high, real_low, imag_low], axis=1)


def turned(value, part_width):
    parts = [value[:, at : at + part_width] for at in range(0, value.shape[1], part_width)]
    return jnp.concatenate(
        [part for at in range(0, len(parts), 2) for part in (-parts[at + 1], parts[at])], axis=1
    )


def right_parts(value):
    high, low = halves(value)
    turned_high, turned_low = (turned(part, value.shape[1] // 2) for part in (high, low))
    return jnp.concatenate([high, turned_high, low, turned_low, high, turned_high], axis=0)


def whereabouts():
    row, col = lax.axis_index("row"), lax.axis_index("col")
    return row * lax.axis_size("col") + col, row // 2, lax.rem(row, 2), col // RING, lax.rem(col, RING)


def running_count(mask):
    length = mask.shape[1]
    former = lax.broadcasted_iota(jnp.int32, (length, length), 0)
    latter = lax.broadcasted_iota(jnp.int32, (length, length), 1)
    upto = jnp.where(former <= latter, 1.0, 0.0).astype(BF16)
    return dot(mask.astype(BF16), upto)


def leaf_kernel(
    count_ref, owner_hbm, source_hbm, inv_hbm, low_hbm, out_ref, owner_ref, source_ref, inv_ref, low_ref, sems
):
    devices, contrib = owner_hbm.shape[0], owner_ref.shape[1]
    myself = whereabouts()[0]
    pivots, breadth = inv_ref.shape[1], source_ref.shape[2]
    groups = 2 * breadth // LANES
    copies = [
        pltpu.make_async_copy(former, latter, sems.at[i])
        for i, (former, latter) in enumerate(
            (
                (source_hbm, source_ref),
                (inv_hbm, inv_ref),
                (owner_hbm.at[myself], owner_ref),
                (low_hbm, low_ref),
            )
        )
    ]
    for copy in copies:
        copy.start()
    copies[2].wait()
    names = lax.broadcasted_iota(jnp.int32, (devices, contrib), 0)
    position = lax.broadcasted_iota(jnp.int32, (devices, contrib), 1)
    chosen = jnp.where((names == owner_ref[...]) & (position < count_ref[myself]), 1.0, 0.0)
    rank = running_count(chosen) * chosen
    pick = jnp.concatenate(
        [jnp.where(rank == k + 1.0, 1.0, 0.0).astype(BF16) for k in range(CAPACITY)], axis=0
    )
    copies[0].wait()
    pivot_source = jnp.concatenate([source_ref[0, :pivots], source_ref[1, :pivots]], axis=1)
    copies[1].wait()
    half = pivots // 2
    upper = dot(
        left_parts(inv_ref[0, :half, :half], inv_ref[1, :half, :half]), right_parts(pivot_source[:half])
    )
    lower = dot(left_parts(inv_ref[0, half:], inv_ref[1, half:]), right_parts(pivot_source))
    pivot_part = jnp.concatenate([upper, lower], axis=0)
    copies[3].wait()
    eliminated = dot(left_parts(low_ref[0], low_ref[1]), right_parts(pivot_part))
    update = jnp.concatenate([source_ref[0, pivots:], source_ref[1, pivots:]], axis=1) - eliminated
    high, low = halves(update)
    rows = dot(jnp.concatenate([pick, pick], axis=1), jnp.concatenate([high, low], axis=0))
    for k in range(CAPACITY):
        for g in range(groups):
            at = (g % 2) * breadth + g // 2 * LANES
            out_ref[pl.ds(k * groups + g, devices, stride=CAPACITY * groups), :] = rows[
                k * devices : (k + 1) * devices, at : at + LANES
            ]


def placing_kernel(owner_ref, slot_ref, token_hbm, out_ref):
    del token_hbm
    devices = owner_ref.shape[0]
    owned = out_ref.shape[2]
    mine = jnp.where(owner_ref[...] == whereabouts()[0], 1.0, 0.0)
    rank = running_count(mine) * mine
    slots = slot_ref[...].astype(F32) + 1.0
    rows = lax.broadcasted_iota(jnp.int32, (devices, owned), 1).astype(F32) + 1.0
    for k in range(CAPACITY):
        slot = jnp.sum(jnp.where(rank == k + 1.0, slots, 0.0), axis=1, keepdims=True)
        out_ref[k] = jnp.where(slot == rows, 1.0, 0.0).astype(BF16)


def extend_kernel(placing_ref, arrived_ref, parent_ref, out_ref):
    devices = placing_ref.shape[1]
    groups = out_ref.shape[1] // LANES
    for g in range(groups):
        total = parent_ref[g % 2, :, g // 2 * LANES : (g // 2 + 1) * LANES]
        for k in range(CAPACITY):
            rows = arrived_ref[pl.ds(k * groups + g, devices, stride=CAPACITY * groups), :]
            high, low = halves(rows)
            total += dot(placing_ref[k], high, ((0,), (0,)))
            total += dot(placing_ref[k], low, ((0,), (0,)))
        out_ref[:, g * LANES : (g + 1) * LANES] = total


def first_unit(band, strip=0):
    return 2 * band * (band + 1) + strip * (band + 1)


UNITS = first_unit(RING)


def split_kernel(value_ref, after_hbm, out_ref, token_ref):
    del after_hbm
    token_ref[...] = jnp.zeros_like(token_ref)
    step = pl.program_id(0)
    rows, columns = out_ref.shape[3:]
    strips = value_ref.shape[1] // rows
    steps = RING // strips
    for band in range(RING):

        @pl.when(step // steps == band)
        def _(band=band):
            for j in range(strips):
                strip = lax.rem(step, steps) * strips + j
                for piece in range(band + 1):
                    for part in range(2):
                        value = value_ref[part, j * rows : (j + 1) * rows, piece * columns : (piece + 1) * columns]
                        high, low = halves(value)
                        out_ref[first_unit(band, strip) + piece, 0, part] = high
                        out_ref[first_unit(band, strip) + piece, 1, part] = low


def band_product(held, right_ref, band, strips):
    deep = (band + 1) * held.shape[4]

    def rows(kind, part):
        return jnp.concatenate(
            [
                jnp.concatenate([held[first_unit(band, strip) + piece, kind, part] for piece in range(band + 1)], axis=1)
                for strip in strips
            ],
            axis=0,
        )

    left = [[rows(kind, part) for part in range(2)] for kind in range(2)]
    right = [right_ref[kind, :deep] for kind in range(4)]
    return dot(
        jnp.concatenate([left[0][0], left[0][1], left[0][0], left[0][1], left[1][0], left[1][1]], axis=1),
        jnp.concatenate([right[0], right[1], right[2], right[3], right[0], right[1]], axis=0),
    )


def hop_from(own, index):
    return lax.rem(index - own + RING, RING)


def each_copy(units_hbm, held, sems, hops, act):
    _, _, own_core, own_y, own_z = whereabouts()

    def copy(first, count, sem):
        act(pltpu.make_async_copy(units_hbm.at[pl.ds(first, count)], held.at[pl.ds(first, count)], sems.at[sem]))

    for hop in hops:
        for band in range(RING):

            @pl.when((own_core == 0) & (hop_from(own_y, band) == hop))
            def _(band=band):
                copy(first_unit(band), RING * (band + 1), band)

        @pl.when(own_core == 1)
        def _(hop=hop):
            for band in range(RING):
                copy(first_unit(band, lax.rem(own_z + hop, RING)), band + 1, hop * RING + band)


def start_rows(*args):
    each_copy(*args, lambda copy: copy.start())


def wait_rows(*args):
    each_copy(*args, lambda copy: copy.wait())


def product_by_hop(held, right_ref, hops, store):
    owned = held.shape[3]
    _, _, own_core, own_y, own_z = whereabouts()
    for band in range(RING):
        for hop in hops:

            @pl.when((own_core == 0) & (hop_from(own_y, band) == hop))
            def _(band=band, hop=hop):
                result = band_product(held, right_ref, band, range(RING))
                for strip in range(RING):
                    store(hop, hop_from(own_z, strip), result[strip * owned : (strip + 1) * owned])

        @pl.when(own_core == 1)
        def _(band=band):
            result = band_product(held, right_ref, band, [lax.rem(own_z + hop, RING) for hop in hops])
            for at, hop in enumerate(hops):
                store(hop, hop_from(own_y, band), result[at * owned : (at + 1) * owned])


def far_kernel(
    units_hbm, own_ref, other_ref, left_ref, right_ref, far_ref, left2_ref, right2_ref, far2_ref,
    right_side, to_left, to_right, held, sems,
):
    owned = own_ref.shape[0]
    _, own_x, own_core, _, _ = whereabouts()

    def fill():
        for hop, ref, ref2 in (
            (0, own_ref, other_ref), (1, left_ref, left2_ref), (3, right_ref, right2_ref), (2, far_ref, far2_ref)
        ):
            for core, piece in ((own_core, ref), (1 - own_core, ref2)):
                at = pl.multiple_of((hop_from(hop, own_x) * 2 + core) * owned, owned)
                high, low = halves(piece[...])
                for kind, value in enumerate((high, turned(high, SOURCES), low, turned(low, SOURCES))):
                    right_side[kind, pl.ds(at, owned), :] = value

    def store(hop, other_hop, value):
        for at, ref in enumerate((to_left, to_right)):

            @pl.when(other_hop // 2 == at)
            def _(ref=ref):
                ref[lax.rem(other_hop, 2)] = value

    start_rows(units_hbm, held, sems, (2,))
    start_rows(units_hbm, held, sems, (1, 3, 0))
    fill()
    wait_rows(units_hbm, held, sems, (2,))
    product_by_hop(held, right_side, (2,), store)
    wait_rows(units_hbm, held, sems, (1, 3, 0))


def near_kernel(held, right_side, left, right):
    def store(hop, other_hop, value):
        (left if hop == 1 else right)[other_hop] = value

    product_by_hop(held, right_side, (1, 3), store)


def own_kernel(held, right_side, own):
    def store(hop, other_hop, value):
        own[other_hop] = value

    product_by_hop(held, right_side, (0,), store)


def join_kernel(left, right, got_left, got_right, *outs):
    for hops, (left_out, right_out) in zip(BATCHES, (outs[:2], outs[2:])):
        for at, hop in enumerate(hops):
            left_out[at] = left[hop] + got_left[hop] if hop < 2 else left[hop]
            right_out[at] = right[hop] + got_right[hop - 2] if hop >= 2 else right[hop]


def settle_kernel(hops, own, got_left, got_right, *outs):
    for at, (hop, out) in enumerate(zip(hops, outs)):
        out[...] = own[hop] + got_left[at] + got_right[at]


def material_gradient(eliminated, kernel_coef, p_speed, s_speed, density):
    norming = 1.0 / jnp.sqrt(jnp.float32(SOURCES))
    fwd_real, fwd_imag, adj_real, adj_imag = (eliminated[:, at * SOURCES : (at + 1) * SOURCES] for at in range(4))
    k_lambda = jnp.sum(fwd_real * adj_real - fwd_imag * adj_imag, axis=1) * norming
    k_mu = jnp.sum(fwd_real * adj_imag + fwd_imag * adj_real, axis=1) * norming
    k_rho = jnp.sum(fwd_real * adj_real + fwd_imag * adj_imag, axis=1) * norming
    grad_lambda = kernel_coef[0] * k_lambda
    grad_mu = kernel_coef[1] * k_mu
    grad_rho = kernel_coef[2] * k_rho
    first_out = 2.0 * density * p_speed * grad_lambda
    second_out = 2.0 * density * s_speed * (grad_mu - 2.0 * grad_lambda)
    third_out = (
        (p_speed * p_speed - 2.0 * s_speed * s_speed) * grad_lambda
        + s_speed * s_speed * grad_mu
        + grad_rho
    )
    return jnp.stack([first_out, second_out, third_out])


def along(axis, hop):
    if axis == "core":
        return [(i, i ^ 1) for i in range(2 * RING)]
    if axis == "x":
        return [(i, (i + 2 * hop) % (2 * RING)) for i in range(2 * RING)]
    if axis == "y":
        return [(i, (i + RING * hop) % (RING * RING)) for i in range(RING * RING)]
    return [(i, i // RING * RING + (i + hop) % RING) for i in range(RING * RING)]


def move(value, axis, hop=1):
    return lax.ppermute(value, "row" if axis in ("x", "core") else "col", along(axis, hop))


def move_by_core(value, phase, hop):
    pairs = []
    for row in range(2 * RING):
        axis = "yz"[(row + phase) % 2]
        pairs += [(row * RING * RING + former, row * RING * RING + latter) for former, latter in along(axis, hop)]
    return lax.ppermute(value, ("row", "col"), pairs)


def params(mebibytes, **more):
    return pltpu.CompilerParams(vmem_limit_bytes=mebibytes << 20, **more)


SMEM = pl.BlockSpec(memory_space=pltpu.SMEM)
VMEM = pl.BlockSpec(memory_space=pltpu.VMEM)
ANY = pl.BlockSpec(memory_space=pl.ANY)


def per_device(
    leaf_source,
    leaf_inv,
    leaf_low,
    child_count,
    child_owner,
    child_slot,
    parent_source,
    parent_inv,
    kernel_coef,
    p_speed,
    s_speed,
    density,
):
    devices = lax.axis_size("row") * lax.axis_size("col")
    owned = parent_source.shape[1]
    width = 2 * parent_source.shape[2]
    contrib = child_slot.shape[1]
    position = jnp.arange(contrib, dtype=jnp.int32)
    owner = jnp.where(position[None, :] < child_count[:, None], child_owner[:, :, 0], -1)

    outgoing = pl.pallas_call(
        leaf_kernel,
        out_shape=jax.ShapeDtypeStruct((devices * CAPACITY * width // LANES, LANES), F32),
        in_specs=[SMEM] + [ANY] * 4,
        out_specs=VMEM,
        scratch_shapes=[
            pltpu.VMEM((1, contrib), jnp.int32),
            pltpu.VMEM((2,) + leaf_source.shape[2:], F32),
            pltpu.VMEM(leaf_inv.shape[1:], F32),
            pltpu.VMEM(leaf_low.shape[1:], F32),
            pltpu.SemaphoreType.DMA((4,)),
        ],
        compiler_params=params(60),
        name="leaf",
    )(child_count, child_owner.reshape(devices, 1, contrib), leaf_source[:, 0], leaf_inv[0], leaf_low[0])
    rows, depth = parent_inv.shape[1:]
    block = rows // 8
    block_spec = pl.BlockSpec((2, block, depth), lambda i: (0, i, 0))
    units_shape = jax.ShapeDtypeStruct((UNITS, 2, 2, owned, depth // RING), BF16)
    units, token = pl.pallas_call(
        split_kernel,
        out_shape=[units_shape, jax.ShapeDtypeStruct((8, LANES), F32)],
        grid=(rows // block,),
        in_specs=[block_spec, ANY],
        out_specs=[pl.BlockSpec(units_shape.shape, lambda i: (0,) * 5), pl.BlockSpec((8, LANES), lambda i: (0, 0))],
        compiler_params=params(60),
        cost_estimate=pl.CostEstimate(flops=4 * rows * depth, bytes_accessed=16 * rows * depth, transcendentals=0),
        name="split",
    )(parent_inv, outgoing)
    placing = pl.pallas_call(
        placing_kernel,
        out_shape=jax.ShapeDtypeStruct((CAPACITY, devices, owned), BF16),
        in_specs=[VMEM] * 2 + [ANY],
        out_specs=VMEM,
        compiler_params=params(16),
        cost_estimate=pl.CostEstimate(flops=2 * devices * 512 * 512, bytes_accessed=1 << 20, transcendentals=0),
        name="placing",
    )(owner, child_slot, token)
    arrived = lax.all_to_all(
        outgoing.reshape(devices, -1, LANES), ("row", "col"), split_axis=0, concat_axis=0, tiled=True
    )
    assembled = pl.pallas_call(
        extend_kernel,
        out_shape=jax.ShapeDtypeStruct((owned, width), F32),
        in_specs=[VMEM] * 3,
        out_specs=VMEM,
        compiler_params=params(16),
        name="extend",
    )(placing, arrived.reshape(outgoing.shape), parent_source)

    other = move(assembled, "core")
    hops = [move(assembled, "x", hop) for hop in (1, 3, 2)]
    swapped = [move(value, "core") for value in hops]

    two = jax.ShapeDtypeStruct((2, owned, width), F32)
    four = jax.ShapeDtypeStruct((RING, owned, width), F32)

    def cost(blocks):
        return pl.CostEstimate(flops=blocks * 6 * rows * depth * width, bytes_accessed=1 << 20, transcendentals=0)

    right_side, to_left, to_right, held = pl.pallas_call(
        far_kernel,
        out_shape=[jax.ShapeDtypeStruct((4, depth, width), BF16), two, two, units_shape],
        in_specs=[ANY] + [VMEM] * 8,
        out_specs=[VMEM] * 4,
        scratch_shapes=[pltpu.SemaphoreType.DMA((RING * RING,))],
        compiler_params=params(33),
        name="far",
    )(units, assembled, other, *hops, *swapped)
    got_left, got_right = move_by_core(to_left, 0, 1), move_by_core(to_right, 0, 3)
    left, right = pl.pallas_call(
        near_kernel,
        out_shape=[four] * 2,
        in_specs=[VMEM] * 2,
        out_specs=[VMEM] * 2,
        compiler_params=params(36),
        cost_estimate=cost(2),
        name="near",
    )(held, right_side)
    joined = pl.pallas_call(
        join_kernel,
        out_shape=[two] * 4,
        in_specs=[VMEM] * 4,
        out_specs=[VMEM] * 4,
        compiler_params=params(16),
        name="join",
    )(left, right, got_left, got_right)
    got = [move_by_core(value, 0, (1, 3)[at % 2]) for at, value in enumerate(joined)]
    own = pl.pallas_call(
        own_kernel,
        out_shape=four,
        in_specs=[VMEM] * 2,
        out_specs=VMEM,
        compiler_params=params(36),
        cost_estimate=cost(1),
        name="own",
    )(held, right_side)
    parts = []
    for at, hops in enumerate(BATCHES):
        values = pl.pallas_call(
            functools.partial(settle_kernel, hops),
            out_shape=[jax.ShapeDtypeStruct((owned, width), F32)] * 2,
            in_specs=[VMEM] * 3,
            out_specs=[VMEM] * 2,
            compiler_params=params(16),
            name="settle",
        )(own, got[2 * at], got[2 * at + 1])
        parts += [move_by_core(value, 1, hop) if hop else value for value, hop in zip(values, hops)]
    eliminated = functools.reduce(jnp.add, parts)
    return material_gradient(eliminated, kernel_coef, p_speed, s_speed, density)


def solution(mesh):
    return jax.shard_map(
        per_device,
        mesh=mesh,
        in_specs=(
            P(None, ("row", "col"), None, None),
            P(("row", "col"), None, None, None),
            P(("row", "col"), None, None, None),
            P(),
            P(),
            P(),
            P(None, ("row", "col"), None),
            P(None, "row", "col"),
            P(None, ("row", "col")),
            P(("row", "col")),
            P(("row", "col")),
            P(("row", "col")),
        ),
        out_specs=P(None, ("row", "col")),
        check_vma=False,
    )
```

profile of v0, /device:TPU:0, one launch (start us, length us, event | category | flops | bytes accessed | tf_op | source)
XLA Modules:
  0.0 105.1 jit_solution(11518004082999585479)
XLA Ops:
  0.0 8.2 %leaf.1.after_hbm = f32[3072,128]{1,0:T(8,128)} custom-call(s32[128]{0:T(128)} %count_ref.1, s32[128,1,512]{2,1,0:T(1,128)} %bitcast.39, f32[2,1024,256]{2,1,0:T(8,128)} %bitcast.36, f32[2,512,512]{2,1,0:T(8,128)} %bitcast.37, f32[2,512,512]{2,1,0:T(8,128)} %bitcast.38), custom_call_target="tpu_custom_call" | custom-call | tf_op jit(solution)/shard_map/leaf/pallas_call | solution.py:363
  8.2 11.1 %all-to-all-start = ((f32[128,24,128]{2,1,0:T(8,128)}), f32[128,24,128]{2,1,0:T(8,128)S(1)}, u32[]{:S(2)}, u32[]{:S(2)}) async-start(f32[128,24,128]{2,1,0:T(8,128)} %bitcast.35), calls=%async_computation | async-start | bytes 3145728 | tf_op jit(solution)/shard_map/all_to_all | solution.py:401
  19.4 12.2 %split.1 = (bf16[40,2,2,128,256]{4,3,2,1,0:T(8,128)(2,1)}, f32[8,128]{1,0:T(8,128)}) custom-call(f32[2,2048,1024]{2,1,0:T(8,128)} %value_ref.1, f32[3072,128]{1,0:T(8,128)} %leaf.1.after_hbm), custom_call_target="tpu_custom_call" | custom-call | flops 8388608 | bytes 33554432 | tf_op jit(solution)/shard_map/split/pallas_call | solution.py:382
  31.7 0.7 copy-done.2
  32.8 11.0 %all-to-all-done = f32[128,24,128]{2,1,0:T(8,128)S(1)} async-done(((f32[128,24,128]{2,1,0:T(8,128)}), f32[128,24,128]{2,1,0:T(8,128)S(1)}, u32[]{:S(2)}, u32[]{:S(2)}) %all-to-all-start) | async-done | bytes 1572896 | tf_op jit(solution)/shard_map/all_to_all | solution.py:401
  44.4 0.9 collective-permute-start.3
  45.3 2.7 %collective-permute-start.2 = (f32[128,512]{1,0:T(8,128)S(1)}, f32[128,512]{1,0:T(8,128)S(1)}, u32[]{:S(2)}, u32[]{:S(2)}) collective-permute-start(f32[128,512]{1,0:T(8,128)S(1)} %extend.1.own_ref), channel_id=1, source_target_pairs={{0,96},{16,112},{32,0},{48,16},{64,32},{80,48},{96,64},{112,80},{1... | collective-permute-start | bytes 786440 | tf_op jit(solution)/shard_map/ppermute | solution.py:322
  48.0 7.3 %collective-permute-done.3.far_ref = f32[128,512]{1,0:T(8,128)S(1)} collective-permute-done((f32[128,512]{1,0:T(8,128)S(1)}, f32[128,512]{1,0:T(8,128)S(1)}, u32[]{:S(2)}, u32[]{:S(2)}) %collective-permute-start.3) | collective-permute-done | bytes 262176 | tf_op jit(solution)/shard_map/ppermute | solution.py:322
  55.3 2.4 %collective-permute-done.2.right_ref = f32[128,512]{1,0:T(8,128)S(1)} collective-permute-done((f32[128,512]{1,0:T(8,128)S(1)}, f32[128,512]{1,0:T(8,128)S(1)}, u32[]{:S(2)}, u32[]{:S(2)}) %collective-permute-start.2) | collective-permute-done | bytes 262176 | tf_op jit(solution)/shard_map/ppermute | solution.py:322
  57.6 1.1 %collective-permute-done.1.left_ref = f32[128,512]{1,0:T(8,128)S(1)} collective-permute-done((f32[128,512]{1,0:T(8,128)S(1)}, f32[128,512]{1,0:T(8,128)S(1)}, u32[]{:S(2)}, u32[]{:S(2)}) %collective-permute-start.1) | collective-permute-done | bytes 262176 | tf_op jit(solution)/shard_map/ppermute | solution.py:322
  59.2 1.1 %collective-permute-done.4.left2_ref = f32[128,512]{1,0:T(8,128)S(1)} collective-permute-done((f32[128,512]{1,0:T(8,128)S(1)}, f32[128,512]{1,0:T(8,128)S(1)}, u32[]{:S(2)}, u32[]{:S(2)}) %collective-permute-start.4) | collective-permute-done | bytes 262176 | tf_op jit(solution)/shard_map/ppermute | solution.py:322
  60.3 5.0 %far.1 = (bf16[4,1024,512]{2,1,0:T(8,128)(2,1)S(1)}, f32[2,128,512]{2,1,0:T(8,128)S(1)}, f32[2,128,512]{2,1,0:T(8,128)S(1)}, bf16[40,2,2,128,256]{4,3,2,1,0:T(8,128)(2,1)S(1)}) custom-call(bf16[40,2,2,128,256]{4,3,2,1,0:T(8,128)(2,1)} %get-tuple-element.21.units_hbm, f32[128,512]{1,0:T(8,128)S(1)} %extend.1.own_ref, ...), custom_call_target="tpu_custom_call" | custom-call | tf_op jit(solution)/shard_map/far/pallas_call | solution.py:423
  65.3 1.9 %collective-permute-start.7 = (f32[2,128,512]{2,1,0:T(8,128)S(1)}, f32[2,128,512]{2,1,0:T(8,128)S(1)}, u32[]{:S(2)}, u32[]{:S(2)}) collective-permute-start(f32[2,128,512]{2,1,0:T(8,128)S(1)} %get-tuple-element.27), channel_id=1, source_target_pairs={{0,4},{1,5},{2,6},{3,7},{4,8},{5,9},{6,10},{7,11},{8,12},{9,13},{1... | collective-permute-start | bytes 1572872 | tf_op jit(solution)/shard_map/ppermute | solution.py:330
  67.3 1.4 %collective-permute-start.8 = (f32[2,128,512]{2,1,0:T(8,128)S(1)}, f32[2,128,512]{2,1,0:T(8,128)S(1)}, u32[]{:S(2)}, u32[]{:S(2)}) collective-permute-start(f32[2,128,512]{2,1,0:T(8,128)S(1)} %get-tuple-element.28), channel_id=1, source_target_pairs={{0,12},{1,13},{2,14},{3,15},{4,0},{5,1},{6,2},{7,3},{8,4},{9,5},{1... | collective-permute-start | bytes 1572872 | tf_op jit(solution)/shard_map/ppermute | solution.py:330
  68.6 5.4 %near.1 = (f32[4,128,512]{2,1,0:T(8,128)S(1)}, f32[4,128,512]{2,1,0:T(8,128)S(1)}) custom-call(bf16[40,2,2,128,256]{4,3,2,1,0:T(8,128)(2,1)S(1)} %get-tuple-element.23.held, bf16[4,1024,512]{2,1,0:T(8,128)(2,1)S(1)} %get-tuple-element.24.right_side), custom_call_target="tpu_custom_call" | custom-call | flops 12884901888 | bytes 1048576 | tf_op jit(solution)/shard_map/near/pallas_call | solution.py:433
  74.1 1.7 %collective-permute-done.7.got_left = f32[2,128,512]{2,1,0:T(8,128)S(1)} collective-permute-done((f32[2,128,512]{2,1,0:T(8,128)S(1)}, f32[2,128,512]{2,1,0:T(8,128)S(1)}, u32[]{:S(2)}, u32[]{:S(2)}) %collective-permute-start.7) | collective-permute-done | bytes 524320 | tf_op jit(solution)/shard_map/ppermute | solution.py:330
  76.8 3.2 %collective-permute-start.10 = (f32[2,128,512]{2,1,0:T(8,128)S(1)}, f32[2,128,512]{2,1,0:T(8,128)S(1)}, u32[]{:S(2)}, u32[]{:S(2)}) collective-permute-start(f32[2,128,512]{2,1,0:T(8,128)S(1)} %get-tuple-element.30), channel_id=1, source_target_pairs={{0,12},{1,13},{2,14},{3,15},{4,0},{5,1},{6,2},{7,3},{8,4},{9,5},{1... | collective-permute-start | bytes 1572872 | tf_op jit(solution)/shard_map/ppermute | solution.py:330
  79.9 3.2 %collective-permute-start.13 = (f32[2,128,512]{2,1,0:T(8,128)S(1)}, f32[2,128,512]{2,1,0:T(8,128)S(1)}, u32[]{:S(2)}, u32[]{:S(2)}) collective-permute-start(f32[2,128,512]{2,1,0:T(8,128)S(1)} %get-tuple-element.34), channel_id=1, source_target_pairs={{0,12},{1,13},{2,14},{3,15},{4,0},{5,1},{6,2},{7,3},{8,4},{9,5},{1... | collective-permute-start | bytes 1572872 | tf_op jit(solution)/shard_map/ppermute | solution.py:330
  83.2 1.0 own.1
  84.2 2.9 %collective-permute-done.9.got_left = f32[2,128,512]{2,1,0:T(8,128)S(1)} collective-permute-done((f32[2,128,512]{2,1,0:T(8,128)S(1)}, f32[2,128,512]{2,1,0:T(8,128)S(1)}, u32[]{:S(2)}, u32[]{:S(2)}) %collective-permute-start.9) | collective-permute-done | bytes 524320 | tf_op jit(solution)/shard_map/ppermute | solution.py:330
  87.2 1.6 %collective-permute-start.11 = (f32[128,512]{1,0:T(8,128)S(1)}, f32[128,512]{1,0:T(8,128)S(1)}, u32[]{:S(2)}, u32[]{:S(2)}) collective-permute-start(f32[128,512]{1,0:T(8,128)S(1)} %get-tuple-element.31), channel_id=1, source_target_pairs={{0,2},{1,3},{2,0},{3,1},{4,6},{5,7},{6,4},{7,5},{8,10},{9,11},{10,... | collective-permute-start | bytes 786440 | tf_op jit(solution)/shard_map/ppermute | solution.py:330
  88.8 7.6 %collective-permute-done.12.got_left = f32[2,128,512]{2,1,0:T(8,128)S(1)} collective-permute-done((f32[2,128,512]{2,1,0:T(8,128)S(1)}, f32[2,128,512]{2,1,0:T(8,128)S(1)}, u32[]{:S(2)}, u32[]{:S(2)}) %collective-permute-start.12) | collective-permute-done | bytes 524320 | tf_op jit(solution)/shard_map/ppermute | solution.py:330
  97.1 2.7 %collective-permute-start.15 = (f32[128,512]{1,0:T(8,128)S(1)}, f32[128,512]{1,0:T(8,128)S(1)}, u32[]{:S(2)}, u32[]{:S(2)}) collective-permute-start(f32[128,512]{1,0:T(8,128)S(1)} %get-tuple-element.36), channel_id=1, source_target_pairs={{0,3},{1,0},{2,1},{3,2},{4,7},{5,4},{6,5},{7,6},{8,11},{9,8},{10,9... | collective-permute-start | bytes 786440 | tf_op jit(solution)/shard_map/ppermute | solution.py:330
  99.8 4.3 %collective-permute-done.14 = f32[128,512]{1,0:T(8,128)S(1)} collective-permute-done((f32[128,512]{1,0:T(8,128)S(1)}, f32[128,512]{1,0:T(8,128)S(1)}, u32[]{:S(2)}, u32[]{:S(2)}) %collective-permute-start.14) | collective-permute-done | bytes 262176 | tf_op jit(solution)/shard_map/ppermute | solution.py:330
  (43 shorter events, 4.2 us)
Async XLA Ops:
  8.2 35.6 %all-to-all-start = ((f32[128,24,128]{2,1,0:T(8,128)}), f32[128,24,128]{2,1,0:T(8,128)S(1)}, u32[]{:S(2)}, u32[]{:S(2)}) async-start(f32[128,24,128]{2,1,0:T(8,128)} %bitcast.35), calls=%async_computation | async-start | bytes 3145728 | tf_op jit(solution)/shard_map/all_to_all | solution.py:401
  19.4 12.2 %copy-start.3 = (s32[128,512,1]{1,2,0:T(1,128)S(1)}, s32[128,512,1]{1,2,0:T(1,128)}, u32[]{:S(2)}) copy-start(s32[128,512,1]{1,2,0:T(1,128)} %param.16) | copy-start | bytes 786436
  19.4 12.3 %copy-start.1 = (s32[128,512]{1,0:T(8,128)S(1)}, s32[128,512]{1,0:T(8,128)}, u32[]{:S(2)}) copy-start(s32[128,512]{1,0:T(8,128)} %slot_ref.1) | copy-start | bytes 786436
  19.4 24.4 %copy-start = (f32[2,128,256]{2,1,0:T(8,128)S(1)}, f32[2,128,256]{2,1,0:T(8,128)}, u32[]{:S(2)}) copy-start(f32[2,128,256]{2,1,0:T(8,128)} %parent_ref.1) | copy-start | bytes 786436
  44.4 10.8 %collective-permute-start.3 = (f32[128,512]{1,0:T(8,128)S(1)}, f32[128,512]{1,0:T(8,128)S(1)}, u32[]{:S(2)}, u32[]{:S(2)}) collective-permute-start(f32[128,512]{1,0:T(8,128)S(1)} %extend.1.own_ref), channel_id=1, source_target_pairs={{0,64},{16,80},{32,96},{48,112},{64,0},{80,16},{96,32},{112,48},{1... | collective-permute-start | bytes 786440 | tf_op jit(solution)/shard_map/ppermute | solution.py:322
  45.3 12.3 %collective-permute-start.2 = (f32[128,512]{1,0:T(8,128)S(1)}, f32[128,512]{1,0:T(8,128)S(1)}, u32[]{:S(2)}, u32[]{:S(2)}) collective-permute-start(f32[128,512]{1,0:T(8,128)S(1)} %extend.1.own_ref), channel_id=1, source_target_pairs={{0,96},{16,112},{32,0},{48,16},{64,32},{80,48},{96,64},{112,80},{1... | collective-permute-start | bytes 786440 | tf_op jit(solution)/shard_map/ppermute | solution.py:322
  48.0 10.8 %collective-permute-start.1 = (f32[128,512]{1,0:T(8,128)S(1)}, f32[128,512]{1,0:T(8,128)S(1)}, u32[]{:S(2)}, u32[]{:S(2)}) collective-permute-start(f32[128,512]{1,0:T(8,128)S(1)} %extend.1.own_ref), channel_id=1, source_target_pairs={{0,32},{16,48},{32,64},{48,80},{64,96},{80,112},{96,0},{112,16},{1... | collective-permute-start | bytes 786440 | tf_op jit(solution)/shard_map/ppermute | solution.py:322
  48.0 10.8 %collective-permute-start = (f32[128,512]{1,0:T(8,128)S(1)}, f32[128,512]{1,0:T(8,128)S(1)}, u32[]{:S(2)}, u32[]{:S(2)}) collective-permute-start(f32[128,512]{1,0:T(8,128)S(1)} %extend.1.own_ref), channel_id=1, source_target_pairs={{0,16},{16,0},{32,48},{48,32},{64,80},{80,64},{96,112},{112,96},{1... | collective-permute-start | bytes 786440 | tf_op jit(solution)/shard_map/ppermute | solution.py:322
  55.3 3.5 %collective-permute-start.6 = (f32[128,512]{1,0:T(8,128)S(1)}, f32[128,512]{1,0:T(8,128)S(1)}, u32[]{:S(2)}, u32[]{:S(2)}) collective-permute-start(f32[128,512]{1,0:T(8,128)S(1)} %collective-permute-done.3.far_ref), channel_id=1, source_target_pairs={{0,16},{16,0},{32,48},{48,32},{64,80},{80,64},{96,112},{112,96},{1... | collective-permute-start | bytes 786440 | tf_op jit(solution)/shard_map/ppermute | solution.py:322
  57.6 1.5 %collective-permute-start.5 = (f32[128,512]{1,0:T(8,128)S(1)}, f32[128,512]{1,0:T(8,128)S(1)}, u32[]{:S(2)}, u32[]{:S(2)}) collective-permute-start(f32[128,512]{1,0:T(8,128)S(1)} %collective-permute-done.2.right_ref), channel_id=1, source_target_pairs={{0,16},{16,0},{32,48},{48,32},{64,80},{80,64},{96,112},{112,96},{1... | collective-permute-start | bytes 786440 | tf_op jit(solution)/shard_map/ppermute | solution.py:322
  58.8 1.5 %collective-permute-start.4 = (f32[128,512]{1,0:T(8,128)S(1)}, f32[128,512]{1,0:T(8,128)S(1)}, u32[]{:S(2)}, u32[]{:S(2)}) collective-permute-start(f32[128,512]{1,0:T(8,128)S(1)} %collective-permute-done.1.left_ref), channel_id=1, source_target_pairs={{0,16},{16,0},{32,48},{48,32},{64,80},{80,64},{96,112},{112,96},{1... | collective-permute-start | bytes 786440 | tf_op jit(solution)/shard_map/ppermute | solution.py:322
  65.3 10.5 %collective-permute-start.7 = (f32[2,128,512]{2,1,0:T(8,128)S(1)}, f32[2,128,512]{2,1,0:T(8,128)S(1)}, u32[]{:S(2)}, u32[]{:S(2)}) collective-permute-start(f32[2,128,512]{2,1,0:T(8,128)S(1)} %get-tuple-element.27), channel_id=1, source_target_pairs={{0,4},{1,5},{2,6},{3,7},{4,8},{5,9},{6,10},{7,11},{8,12},{9,13},{1... | collective-permute-start | bytes 1572872 | tf_op jit(solution)/shard_map/ppermute | solution.py:330
  67.3 9.2 %collective-permute-start.8 = (f32[2,128,512]{2,1,0:T(8,128)S(1)}, f32[2,128,512]{2,1,0:T(8,128)S(1)}, u32[]{:S(2)}, u32[]{:S(2)}) collective-permute-start(f32[2,128,512]{2,1,0:T(8,128)S(1)} %get-tuple-element.28), channel_id=1, source_target_pairs={{0,12},{1,13},{2,14},{3,15},{4,0},{5,1},{6,2},{7,3},{8,4},{9,5},{1... | collective-permute-start | bytes 1572872 | tf_op jit(solution)/shard_map/ppermute | solution.py:330
  76.6 10.5 %collective-permute-start.9 = (f32[2,128,512]{2,1,0:T(8,128)S(1)}, f32[2,128,512]{2,1,0:T(8,128)S(1)}, u32[]{:S(2)}, u32[]{:S(2)}) collective-permute-start(f32[2,128,512]{2,1,0:T(8,128)S(1)} %get-tuple-element.29), channel_id=1, source_target_pairs={{0,4},{1,5},{2,6},{3,7},{4,8},{5,9},{6,10},{7,11},{8,12},{9,13},{1... | collective-permute-start | bytes 1572872 | tf_op jit(solution)/shard_map/ppermute | solution.py:330
  76.8 10.3 %collective-permute-start.10 = (f32[2,128,512]{2,1,0:T(8,128)S(1)}, f32[2,128,512]{2,1,0:T(8,128)S(1)}, u32[]{:S(2)}, u32[]{:S(2)}) collective-permute-start(f32[2,128,512]{2,1,0:T(8,128)S(1)} %get-tuple-element.30), channel_id=1, source_target_pairs={{0,12},{1,13},{2,14},{3,15},{4,0},{5,1},{6,2},{7,3},{8,4},{9,5},{1... | collective-permute-start | bytes 1572872 | tf_op jit(solution)/shard_map/ppermute | solution.py:330
  79.9 16.5 %collective-permute-start.12 = (f32[2,128,512]{2,1,0:T(8,128)S(1)}, f32[2,128,512]{2,1,0:T(8,128)S(1)}, u32[]{:S(2)}, u32[]{:S(2)}) collective-permute-start(f32[2,128,512]{2,1,0:T(8,128)S(1)} %get-tuple-element.33), channel_id=1, source_target_pairs={{0,4},{1,5},{2,6},{3,7},{4,8},{5,9},{6,10},{7,11},{8,12},{9,13},{1... | collective-permute-start | bytes 1572872 | tf_op jit(solution)/shard_map/ppermute | solution.py:330
  79.9 16.5 %collective-permute-start.13 = (f32[2,128,512]{2,1,0:T(8,128)S(1)}, f32[2,128,512]{2,1,0:T(8,128)S(1)}, u32[]{:S(2)}, u32[]{:S(2)}) collective-permute-start(f32[2,128,512]{2,1,0:T(8,128)S(1)} %get-tuple-element.34), channel_id=1, source_target_pairs={{0,12},{1,13},{2,14},{3,15},{4,0},{5,1},{6,2},{7,3},{8,4},{9,5},{1... | collective-permute-start | bytes 1572872 | tf_op jit(solution)/shard_map/ppermute | solution.py:330
  87.2 17.3 %copy-start.5 = (f32[3,128]{1,0:T(4,128)S(1)}, f32[3,128]{1,0:T(4,128)}, u32[]{:S(2)}) copy-start(f32[3,128]{1,0:T(4,128)} %param.20) | copy-start | bytes 4612
  87.2 17.3 %copy-start.6 = (f32[128]{0:T(128)S(1)}, f32[128]{0:T(128)}, u32[]{:S(2)}) copy-start(f32[128]{0:T(128)} %param.22) | copy-start | bytes 1540
  87.2 17.3 %copy-start.7 = (f32[128]{0:T(128)S(1)}, f32[128]{0:T(128)}, u32[]{:S(2)}) copy-start(f32[128]{0:T(128)} %param.23) | copy-start | bytes 1540
  87.2 17.3 %copy-start.8 = (f32[128]{0:T(128)S(1)}, f32[128]{0:T(128)}, u32[]{:S(2)}) copy-start(f32[128]{0:T(128)} %param.21) | copy-start | bytes 1540
  87.2 12.6 %collective-permute-start.11 = (f32[128,512]{1,0:T(8,128)S(1)}, f32[128,512]{1,0:T(8,128)S(1)}, u32[]{:S(2)}, u32[]{:S(2)}) collective-permute-start(f32[128,512]{1,0:T(8,128)S(1)} %get-tuple-element.31), channel_id=1, source_target_pairs={{0,2},{1,3},{2,0},{3,1},{4,6},{5,7},{6,4},{7,5},{8,10},{9,11},{10,... | collective-permute-start | bytes 786440 | tf_op jit(solution)/shard_map/ppermute | solution.py:330
  96.5 7.7 %collective-permute-start.14 = (f32[128,512]{1,0:T(8,128)S(1)}, f32[128,512]{1,0:T(8,128)S(1)}, u32[]{:S(2)}, u32[]{:S(2)}) collective-permute-start(f32[128,512]{1,0:T(8,128)S(1)} %get-tuple-element.35), channel_id=1, source_target_pairs={{0,1},{1,2},{2,3},{3,0},{4,5},{5,6},{6,7},{7,4},{8,9},{9,10},{10,1... | collective-permute-start | bytes 786440 | tf_op jit(solution)/shard_map/ppermute | solution.py:330
  97.1 7.0 %collective-permute-start.15 = (f32[128,512]{1,0:T(8,128)S(1)}, f32[128,512]{1,0:T(8,128)S(1)}, u32[]{:S(2)}, u32[]{:S(2)}) collective-permute-start(f32[128,512]{1,0:T(8,128)S(1)} %get-tuple-element.36), channel_id=1, source_target_pairs={{0,3},{1,0},{2,1},{3,2},{4,7},{5,4},{6,5},{7,6},{8,11},{9,8},{10,9... | collective-permute-start | bytes 786440 | tf_op jit(solution)/shard_map/ppermute | solution.py:330
  (2 other events, 12.9 us)
where the time goes:
time: 106 us; the launch traced here: 105 us
  waiting for transfers between devices  40.5 us (38%)
  Pallas kernels  33.3 us (31%)
  starting transfers between devices  29.4 us (28%)
    ppermute x9, waiting for transfers between devices, move_by_core(): return lax.ppermute(value, ('row', 'col'), pairs)  17.2 us
    ppermute x9, starting transfers between devices, move_by_core(): return lax.ppermute(value, ('row', 'col'), pairs)  14.8 us
    ppermute x7, waiting for transfers between devices, move(): lax.ppermute(value, 'row' if axis in ('x', 'core') else 'col', along(axis...  12.3 us
    pallas_call x1, Pallas kernels, per_device(): pl.pallas_call(split_kernel, out_shape=[units_shape, jax.ShapeDtypeStruct...  12.2 us
    all_to_all x1, starting transfers between devices, per_device(): lax.all_to_all(outgoing.reshape(devices, -1, LANES), ('row', 'col'), spli...  11.1 us
    all_to_all x1, waiting for transfers between devices, per_device(): lax.all_to_all(outgoing.reshape(devices, -1, LANES), ('row', 'col'), spli...  11 us
    pallas_call x1, Pallas kernels, per_device(): pl.pallas_call(leaf_kernel, out_shape=jax.ShapeDtypeStruct((devices * CAP...  8.23 us
    pallas_call x1, Pallas kernels, per_device(): pl.pallas_call(near_kernel, out_shape=[four] * 2, in_specs=[VMEM] * 2, ou...  5.43 us
  transfers between devices with their start and end apart: 17, of which 11 were waited for; matrix products, arithmetic and copies ran while one was open for 0% of the time, Pallas kernels for 18%

commit v1 on v0

--- a/solution.py
+++ b/solution.py
@@ -11,7 +11,6 @@
 CAPACITY = 6
 LANES = 128
 RING = 4
-BATCHES = ((2, 0), (1, 3))
 F32 = jnp.float32
 BF16 = jnp.bfloat16
 
@@ -68,15 +67,16 @@
         pltpu.make_async_copy(former, latter, sems.at[i])
         for i, (former, latter) in enumerate(
             (
-                (source_hbm, source_ref),
+                (source_hbm.at[:, pl.ds(0, pivots)], source_ref.at[:, pl.ds(0, pivots)]),
                 (inv_hbm, inv_ref),
                 (owner_hbm.at[myself], owner_ref),
                 (low_hbm, low_ref),
+                (source_hbm.at[:, pl.ds(pivots, contrib)], source_ref.at[:, pl.ds(pivots, contrib)]),
             )
         )
     ]
-    for copy in copies:
-        copy.start()
+    for at in (2, 0, 1, 3, 4):
+        copies[at].start()
     copies[2].wait()
     names = lax.broadcasted_iota(jnp.int32, (devices, contrib), 0)
     position = lax.broadcasted_iota(jnp.int32, (devices, contrib), 1)
@@ -96,6 +96,7 @@
     pivot_part = jnp.concatenate([upper, lower], axis=0)
     copies[3].wait()
     eliminated = dot(left_parts(low_ref[0], low_ref[1]), right_parts(pivot_part))
+    copies[4].wait()
     update = jnp.concatenate([source_ref[0, pivots:], source_ref[1, pivots:]], axis=1) - eliminated
     high, low = halves(update)
     rows = dot(jnp.concatenate([pick, pick], axis=1), jnp.concatenate([high, low], axis=0))
@@ -161,22 +162,16 @@
                         out_ref[first_unit(band, strip) + piece, 1, part] = low
 
 
-def band_product(held, right_ref, band, strips):
-    deep = (band + 1) * held.shape[4]
+def piece_product(held, right_ref, units, piece):
+    depth = held.shape[4]
 
     def rows(kind, part):
-        return jnp.concatenate(
-            [
-                jnp.concatenate([held[first_unit(band, strip) + piece, kind, part] for piece in range(band + 1)], axis=1)
-                for strip in strips
-            ],
-            axis=0,
-        )
-
-    left = [[rows(kind, part) for part in range(2)] for kind in range(2)]
-    right = [right_ref[kind, :deep] for kind in range(4)]
+        return jnp.concatenate([held[unit, kind, part] for unit in units], axis=0)
+
+    high, low = ([rows(kind, part) for part in range(2)] for kind in range(2))
+    right = [right_ref[kind, pl.ds(pl.multiple_of(piece * depth, depth), depth)] for kind in range(4)]
     return dot(
-        jnp.concatenate([left[0][0], left[0][1], left[0][0], left[0][1], left[1][0], left[1][1]], axis=1),
+        jnp.concatenate([high[0], high[1], high[0], high[1], low[0], low[1]], axis=1),
         jnp.concatenate([right[0], right[1], right[2], right[3], right[0], right[1]], axis=0),
     )
 
@@ -212,81 +207,118 @@
     each_copy(*args, lambda copy: copy.wait())
 
 
-def product_by_hop(held, right_ref, hops, store):
+def product_by_hop(held, right_ref, total, hop, store):
     owned = held.shape[3]
     _, _, own_core, own_y, own_z = whereabouts()
-    for band in range(RING):
-        for hop in hops:
-
-            @pl.when((own_core == 0) & (hop_from(own_y, band) == hop))
-            def _(band=band, hop=hop):
-                result = band_product(held, right_ref, band, range(RING))
-                for strip in range(RING):
-                    store(hop, hop_from(own_z, strip), result[strip * owned : (strip + 1) * owned])
-
-        @pl.when(own_core == 1)
-        def _(band=band):
-            result = band_product(held, right_ref, band, [lax.rem(own_z + hop, RING) for hop in hops])
-            for at, hop in enumerate(hops):
-                store(hop, hop_from(own_y, band), result[at * owned : (at + 1) * owned])
+
+    @pl.when(own_core == 0)
+    def _():
+        band = lax.rem(own_y + hop, RING)
+        total[...] = jnp.zeros_like(total)
+
+        def add(piece, carry):
+            units = [first_unit(band, strip) + piece for strip in range(RING)]
+            total[...] += piece_product(held, right_ref, units, piece)
+            return carry
+
+        lax.fori_loop(0, band + 1, add, 0)
+        for strip in range(RING):
+            store(hop, hop_from(own_z, strip), total[strip * owned : (strip + 1) * owned])
+
+    @pl.when(own_core == 1)
+    def _():
+        strip = lax.rem(own_z + hop, RING)
+        for piece in range(RING):
+            units = [first_unit(band, strip) + piece for band in range(piece, RING)]
+            value = piece_product(held, right_ref, units, piece)
+            if piece:
+                total[piece * owned :] += value
+            else:
+                total[...] = value
+        for band in range(RING):
+            store(hop, hop_from(own_y, band), total[band * owned : (band + 1) * owned])
+
+
+def first_axis_odd():
+    _, _, own_core, own_y, own_z = whereabouts()
+    odd_y, odd_z = lax.rem(own_y, 2), lax.rem(own_z, 2)
+    return jnp.where(own_core == 0, odd_y, odd_z), jnp.where(own_core == 0, odd_z, odd_y)
+
+
+def store_turned(refs, which, slot, value):
+    for at, ref in enumerate(refs):
+
+        @pl.when(which == at)
+        def _(ref=ref):
+            ref[slot] = value
 
 
 def far_kernel(
-    units_hbm, own_ref, other_ref, left_ref, right_ref, far_ref, left2_ref, right2_ref, far2_ref,
-    right_side, to_left, to_right, held, sems,
+    units_hbm, own_ref, other_ref, near_ref, next_ref, far_ref, near2_ref, next2_ref, far2_ref,
+    right_side, first, second, held, sems, total,
 ):
     owned = own_ref.shape[0]
     _, own_x, own_core, _, _ = whereabouts()
 
     def fill():
+        odd_x = lax.rem(own_x, 2)
         for hop, ref, ref2 in (
-            (0, own_ref, other_ref), (1, left_ref, left2_ref), (3, right_ref, right2_ref), (2, far_ref, far2_ref)
+            (0, own_ref, other_ref), (1 + 2 * odd_x, near_ref, near2_ref), (3 - 2 * odd_x, next_ref, next2_ref), (2, far_ref, far2_ref)
         ):
             for core, piece in ((own_core, ref), (1 - own_core, ref2)):
-                at = pl.multiple_of((hop_from(hop, own_x) * 2 + core) * owned, owned)
+                at = pl.multiple_of((lax.rem(own_x + hop, RING) * 2 + core) * owned, owned)
                 high, low = halves(piece[...])
                 for kind, value in enumerate((high, turned(high, SOURCES), low, turned(low, SOURCES))):
                     right_side[kind, pl.ds(at, owned), :] = value
 
+    odd, _ = first_axis_odd()
+
     def store(hop, other_hop, value):
-        for at, ref in enumerate((to_left, to_right)):
-
-            @pl.when(other_hop // 2 == at)
-            def _(ref=ref):
-                ref[lax.rem(other_hop, 2)] = value
+        store_turned((first, second), lax.rem(other_hop // 2 + odd, 2), lax.rem(other_hop, 2), value)
 
     start_rows(units_hbm, held, sems, (2,))
     start_rows(units_hbm, held, sems, (1, 3, 0))
     fill()
     wait_rows(units_hbm, held, sems, (2,))
-    product_by_hop(held, right_side, (2,), store)
+    product_by_hop(held, right_side, total, 2, store)
     wait_rows(units_hbm, held, sems, (1, 3, 0))
 
 
-def near_kernel(held, right_side, left, right):
+def near_kernel(way, held, right_side, after_any, free, joined, total):
+    del after_any
+    odd, _ = first_axis_odd()
+    hop = 1 + 2 * lax.rem(way + odd, 2)
+
     def store(hop, other_hop, value):
-        (left if hop == 1 else right)[other_hop] = value
-
-    product_by_hop(held, right_side, (1, 3), store)
-
-
-def own_kernel(held, right_side, own):
+        store_turned((free, joined), jnp.where(other_hop // 2 == hop // 2, 1, 0), lax.rem(other_hop, 2), value)
+
+    product_by_hop(held, right_side, total, hop, store)
+
+
+def own_kernel(held, right_side, first, second, total):
+    odd, _ = first_axis_odd()
+
     def store(hop, other_hop, value):
-        own[other_hop] = value
-
-    product_by_hop(held, right_side, (0,), store)
-
-
-def join_kernel(left, right, got_left, got_right, *outs):
-    for hops, (left_out, right_out) in zip(BATCHES, (outs[:2], outs[2:])):
-        for at, hop in enumerate(hops):
-            left_out[at] = left[hop] + got_left[hop] if hop < 2 else left[hop]
-            right_out[at] = right[hop] + got_right[hop - 2] if hop >= 2 else right[hop]
-
-
-def settle_kernel(hops, own, got_left, got_right, *outs):
-    for at, (hop, out) in enumerate(zip(hops, outs)):
-        out[...] = own[hop] + got_left[at] + got_right[at]
+        store_turned((first, second), lax.rem(other_hop // 2 + odd, 2), lax.rem(other_hop, 2), value)
+
+    product_by_hop(held, right_side, total, 0, store)
+
+
+def settle_kernel(own_first, own_second, first_free, first_joined, second_free, second_joined, *outs):
+    keep, far, near, after = outs
+    odd, other_odd = first_axis_odd()
+    sums = own_first[...] + first_free[...] + second_joined[...], own_second[...] + first_joined[...] + second_free[...]
+    for turn in range(2):
+
+        @pl.when(odd == turn)
+        def _(turn=turn):
+            blocks = [sums[(hop // 2 + turn) % 2][hop % 2] for hop in range(RING)]
+            keep[...], far[...] = blocks[0], blocks[2]
+            for other_turn in range(2):
+
+                @pl.when(other_odd == other_turn)
+                def _(other_turn=other_turn):
+                    near[...], after[...] = blocks[1 + 2 * other_turn], blocks[3 - 2 * other_turn]
 
 
 def material_gradient(eliminated, kernel_coef, p_speed, s_speed, density):
@@ -308,25 +340,27 @@
     return jnp.stack([first_out, second_out, third_out])
 
 
-def along(axis, hop):
-    if axis == "core":
-        return [(i, i ^ 1) for i in range(2 * RING)]
-    if axis == "x":
-        return [(i, (i + 2 * hop) % (2 * RING)) for i in range(2 * RING)]
-    if axis == "y":
-        return [(i, (i + RING * hop) % (RING * RING)) for i in range(RING * RING)]
-    return [(i, i // RING * RING + (i + hop) % RING) for i in range(RING * RING)]
-
-
-def move(value, axis, hop=1):
-    return lax.ppermute(value, "row" if axis in ("x", "core") else "col", along(axis, hop))
-
-
-def move_by_core(value, phase, hop):
+def partner(at, way):
+    return (at + 2) % RING if way == 2 else (at + 1 + 2 * ((at + way) % 2)) % RING
+
+
+def swap_cores(value):
+    return lax.ppermute(value, "row", [(i, i ^ 1) for i in range(2 * RING)])
+
+
+def move_x(value, way):
+    return lax.ppermute(value, "row", [(i, 2 * partner(i // 2, way) + i % 2) for i in range(2 * RING)])
+
+
+def move_by_core(value, phase, way):
     pairs = []
-    for row in range(2 * RING):
-        axis = "yz"[(row + phase) % 2]
-        pairs += [(row * RING * RING + former, row * RING * RING + latter) for former, latter in along(axis, hop)]
+    for former in range(2 * RING**3):
+        row, y, z = former // RING**2, former // RING % RING, former % RING
+        if (row + phase) % 2:
+            z = partner(z, way)
+        else:
+            y = partner(y, way)
+        pairs.append((former, (row * RING + y) * RING + z))
     return lax.ppermute(value, ("row", "col"), pairs)
 
 
@@ -370,7 +404,7 @@
             pltpu.VMEM((2,) + leaf_source.shape[2:], F32),
             pltpu.VMEM(leaf_inv.shape[1:], F32),
             pltpu.VMEM(leaf_low.shape[1:], F32),
-            pltpu.SemaphoreType.DMA((4,)),
+            pltpu.SemaphoreType.DMA((5,)),
         ],
         compiler_params=params(60),
         name="leaf",
@@ -410,65 +444,64 @@
         name="extend",
     )(placing, arrived.reshape(outgoing.shape), parent_source)
 
-    other = move(assembled, "core")
-    hops = [move(assembled, "x", hop) for hop in (1, 3, 2)]
-    swapped = [move(value, "core") for value in hops]
+    other = swap_cores(assembled)
+    hops = [move_x(assembled, way) for way in range(3)]
+    swapped = [swap_cores(value) for value in hops]
 
     two = jax.ShapeDtypeStruct((2, owned, width), F32)
-    four = jax.ShapeDtypeStruct((RING, owned, width), F32)
+
+    total = pltpu.VMEM((RING * owned, width), F32)
 
     def cost(blocks):
         return pl.CostEstimate(flops=blocks * 6 * rows * depth * width, bytes_accessed=1 << 20, transcendentals=0)
 
-    right_side, to_left, to_right, held = pl.pallas_call(
+    right_side, first, second, held = pl.pallas_call(
         far_kernel,
         out_shape=[jax.ShapeDtypeStruct((4, depth, width), BF16), two, two, units_shape],
         in_specs=[ANY] + [VMEM] * 8,
         out_specs=[VMEM] * 4,
-        scratch_shapes=[pltpu.SemaphoreType.DMA((RING * RING,))],
+        scratch_shapes=[pltpu.SemaphoreType.DMA((RING * RING,)), total],
         compiler_params=params(33),
         name="far",
     )(units, assembled, other, *hops, *swapped)
-    got_left, got_right = move_by_core(to_left, 0, 1), move_by_core(to_right, 0, 3)
-    left, right = pl.pallas_call(
-        near_kernel,
-        out_shape=[four] * 2,
+    got_first, got_second = move_by_core(first, 0, 0), move_by_core(second, 0, 1)
+
+    def near(way, after):
+        return pl.pallas_call(
+            functools.partial(near_kernel, way),
+            out_shape=[two] * 2,
+            in_specs=[VMEM] * 2 + [ANY],
+            out_specs=[VMEM] * 2,
+            scratch_shapes=[total],
+            compiler_params=params(36),
+            cost_estimate=cost(1),
+            name="near",
+        )(held, right_side, after)
+
+    first_free, first_joined = near(0, first)
+    second_free, second_joined = near(1, first_joined)
+    first_free, second_free = move_by_core(first_free, 0, 0), move_by_core(second_free, 0, 1)
+    first_joined = move_by_core(first_joined + got_second, 0, 0)
+    second_joined = move_by_core(second_joined + got_first, 0, 1)
+    own = pl.pallas_call(
+        own_kernel,
+        out_shape=[two] * 2,
         in_specs=[VMEM] * 2,
         out_specs=[VMEM] * 2,
-        compiler_params=params(36),
-        cost_estimate=cost(2),
-        name="near",
-    )(held, right_side)
-    joined = pl.pallas_call(
-        join_kernel,
-        out_shape=[two] * 4,
-        in_specs=[VMEM] * 4,
-        out_specs=[VMEM] * 4,
-        compiler_params=params(16),
-        name="join",
-    )(left, right, got_left, got_right)
-    got = [move_by_core(value, 0, (1, 3)[at % 2]) for at, value in enumerate(joined)]
-    own = pl.pallas_call(
-        own_kernel,
-        out_shape=four,
-        in_specs=[VMEM] * 2,
-        out_specs=VMEM,
+        scratch_shapes=[total],
         compiler_params=params(36),
         cost_estimate=cost(1),
         name="own",
     )(held, right_side)
-    parts = []
-    for at, hops in enumerate(BATCHES):
-        values = pl.pallas_call(
-            functools.partial(settle_kernel, hops),
-            out_shape=[jax.ShapeDtypeStruct((owned, width), F32)] * 2,
-            in_specs=[VMEM] * 3,
-            out_specs=[VMEM] * 2,
-            compiler_params=params(16),
-            name="settle",
-        )(own, got[2 * at], got[2 * at + 1])
-        parts += [move_by_core(value, 1, hop) if hop else value for value, hop in zip(values, hops)]
-    eliminated = functools.reduce(jnp.add, parts)
+    keep, far, closest, after = pl.pallas_call(
+        settle_kernel,
+        out_shape=[jax.ShapeDtypeStruct((owned, width), F32)] * 4,
+        in_specs=[VMEM] * 6,
+        out_specs=[VMEM] * 4,
+        compiler_params=params(16),
+        name="settle",
+    )(*own, first_free, first_joined, second_free, second_joined)
+    eliminated = keep + move_by_core(far, 1, 2) + move_by_core(closest, 1, 0) + move_by_core(after, 1, 1)
     return material_gradient(eliminated, kernel_coef, p_speed, s_speed, density)
 
 

time: 106 us -> 103 us (0.972)
  starting transfers between devices: 29.4 us -> 26.7 us
  Pallas kernels: 33.3 us -> 34.5 us
    ppermute x9, starting transfers between devices: 14.8 us -> 11.4 us  [move_by_core(): return lax.ppermute(value, ('row', 'col'), pairs)]
    pallas_call x5 -> x4, Pallas kernels: 6.77 us -> 7.91 us  [the longest x2 6.47 us: near(): pl.pallas_call(functools.partial(near_kernel, way), out_shape=[two] * 2,...]
  transfers between devices with their start and end apart: 17 -> 17, of which waited for: 11 -> 10; matrix products, arithmetic and copies ran while one was open for 0% -> 0% of each run, Pallas kernels for 18% -> 20%
where the time goes in v1:
time: 103 us
  waiting for transfers between devices  39.6 us (38%)
  Pallas kernels  34.5 us (33%)
  starting transfers between devices  26.7 us (26%)
  other arithmetic  1.07 us (1%)
    ppermute x9, waiting for transfers between devices, move_by_core(): return lax.ppermute(value, ('row', 'col'), pairs)  16.4 us
    pallas_call x1, Pallas kernels, per_device(): pl.pallas_call(split_kernel, out_shape=[units_shape, jax.ShapeDtypeStruct...  12.2 us
    ppermute x9, starting transfers between devices, move_by_core(): return lax.ppermute(value, ('row', 'col'), pairs)  11.4 us
    all_to_all x1, starting transfers between devices, per_device(): lax.all_to_all(outgoing.reshape(devices, -1, LANES), ('row', 'col'), spli...  11.1 us
    all_to_all x1, waiting for transfers between devices, per_device(): lax.all_to_all(outgoing.reshape(devices, -1, LANES), ('row', 'col'), spli...  11 us
    ppermute x3, waiting for transfers between devices, move_x(): lax.ppermute(value, 'row', [(i, 2 * partner(i // 2, way) + i % 2) for i i...  10.8 us
    pallas_call x1, Pallas kernels, per_device(): pl.pallas_call(leaf_kernel, out_shape=jax.ShapeDtypeStruct((devices * CAP...  8.06 us
    pallas_call x2, Pallas kernels, near(): pl.pallas_call(functools.partial(near_kernel, way), out_shape=[two] * 2,...  6.47 us
  transfers between devices with their start and end apart: 17, of which 10 were waited for; matrix products, arithmetic and copies ran while one was open for 0% of the time, Pallas kernels for 20%

profile of v1, /device:TPU:0, one launch (start us, length us, event | category | flops | bytes accessed | tf_op | source)
XLA Modules:
  0.0 102.7 jit_solution(14756625437844386122)
XLA Ops:
  0.0 8.1 %leaf.1.after_hbm = f32[3072,128]{1,0:T(8,128)} custom-call(s32[128]{0:T(128)} %count_ref.1, s32[128,1,512]{2,1,0:T(1,128)} %bitcast.39, f32[2,1024,256]{2,1,0:T(8,128)} %bitcast.36, f32[2,512,512]{2,1,0:T(8,128)} %bitcast.37, f32[2,512,512]{2,1,0:T(8,128)} %bitcast.38), custom_call_target="tpu_custom_call" | custom-call | tf_op jit(solution)/shard_map/leaf/pallas_call | solution.py:397
  8.1 11.1 %all-to-all-start = ((f32[128,24,128]{2,1,0:T(8,128)}), f32[128,24,128]{2,1,0:T(8,128)S(1)}, u32[]{:S(2)}, u32[]{:S(2)}) async-start(f32[128,24,128]{2,1,0:T(8,128)} %bitcast.35), calls=%async_computation | async-start | bytes 3145728 | tf_op jit(solution)/shard_map/all_to_all | solution.py:435
  19.3 12.2 %split.1 = (bf16[40,2,2,128,256]{4,3,2,1,0:T(8,128)(2,1)}, f32[8,128]{1,0:T(8,128)}) custom-call(f32[2,2048,1024]{2,1,0:T(8,128)} %value_ref.1, f32[3072,128]{1,0:T(8,128)} %leaf.1.after_hbm), custom_call_target="tpu_custom_call" | custom-call | flops 8388608 | bytes 33554432 | tf_op jit(solution)/shard_map/split/pallas_call | solution.py:416
  32.7 11.0 %all-to-all-done = f32[128,24,128]{2,1,0:T(8,128)S(1)} async-done(((f32[128,24,128]{2,1,0:T(8,128)}), f32[128,24,128]{2,1,0:T(8,128)S(1)}, u32[]{:S(2)}, u32[]{:S(2)}) %all-to-all-start) | async-done | bytes 1572896 | tf_op jit(solution)/shard_map/all_to_all | solution.py:435
  44.3 0.9 collective-permute-start.3
  45.2 2.7 %collective-permute-start.2 = (f32[128,512]{1,0:T(8,128)S(1)}, f32[128,512]{1,0:T(8,128)S(1)}, u32[]{:S(2)}, u32[]{:S(2)}) collective-permute-start(f32[128,512]{1,0:T(8,128)S(1)} %extend.1.own_ref), channel_id=1, source_target_pairs={{0,96},{16,112},{32,64},{48,80},{64,32},{80,48},{96,0},{112,16},{1... | collective-permute-start | bytes 786440 | tf_op jit(solution)/shard_map/ppermute | solution.py:352
  47.9 7.3 %collective-permute-done.3.far_ref = f32[128,512]{1,0:T(8,128)S(1)} collective-permute-done((f32[128,512]{1,0:T(8,128)S(1)}, f32[128,512]{1,0:T(8,128)S(1)}, u32[]{:S(2)}, u32[]{:S(2)}) %collective-permute-start.3) | collective-permute-done | bytes 262176 | tf_op jit(solution)/shard_map/ppermute | solution.py:352
  55.2 3.5 %collective-permute-done.2.next_ref = f32[128,512]{1,0:T(8,128)S(1)} collective-permute-done((f32[128,512]{1,0:T(8,128)S(1)}, f32[128,512]{1,0:T(8,128)S(1)}, u32[]{:S(2)}, u32[]{:S(2)}) %collective-permute-start.2) | collective-permute-done | bytes 262176 | tf_op jit(solution)/shard_map/ppermute | solution.py:352
  59.2 1.0 collective-permute-done.5.next2_ref
  60.6 5.3 %far.1 = (bf16[4,1024,512]{2,1,0:T(8,128)(2,1)S(1)}, f32[2,128,512]{2,1,0:T(8,128)S(1)}, f32[2,128,512]{2,1,0:T(8,128)S(1)}, bf16[40,2,2,128,256]{4,3,2,1,0:T(8,128)(2,1)S(1)}) custom-call(bf16[40,2,2,128,256]{4,3,2,1,0:T(8,128)(2,1)} %get-tuple-element.21.units_hbm, f32[128,512]{1,0:T(8,128)S(1)} %extend.1.own_ref, ...), custom_call_target="tpu_custom_call" | custom-call | tf_op jit(solution)/shard_map/far/pallas_call | solution.py:458
  66.5 1.7 %collective-permute-start.11 = (f32[2,128,512]{2,1,0:T(8,128)S(1)}, f32[2,128,512]{2,1,0:T(8,128)S(1)}, u32[]{:S(2)}, u32[]{:S(2)}) collective-permute-start(f32[2,128,512]{2,1,0:T(8,128)S(1)} %get-tuple-element.27.after_any), channel_id=1, source_target_pairs={{0,4},{1,5},{2,6},{3,7},{4,0},{5,1},{6,2},{7,3},{8,12},{9,13},{10,... | collective-permute-start | bytes 1572872 | tf_op jit(solution)/shard_map/ppermute | solution.py:364
  68.2 2.3 %near.2 = (f32[2,128,512]{2,1,0:T(8,128)S(1)}, f32[2,128,512]{2,1,0:T(8,128)S(1)}) custom-call(bf16[40,2,2,128,256]{4,3,2,1,0:T(8,128)(2,1)S(1)} %get-tuple-element.23.held, bf16[4,1024,512]{2,1,0:T(8,128)(2,1)S(1)} %get-tuple-element.24.right_side, f32[2,128,512]{2,1,0:T(8,128)S(1)} %get-tuple-element.27.after_any), custom_call_target="tpu_custom_call" | custom-call | flops 6442450944 | bytes 1048576 | tf_op jit(solution)/shard_map/near/pallas_call | solution.py:470
  70.6 4.1 %near.3 = (f32[2,128,512]{2,1,0:T(8,128)S(1)}, f32[2,128,512]{2,1,0:T(8,128)S(1)}) custom-call(bf16[40,2,2,128,256]{4,3,2,1,0:T(8,128)(2,1)S(1)} %get-tuple-element.23.held, bf16[4,1024,512]{2,1,0:T(8,128)(2,1)S(1)} %get-tuple-element.24.right_side, f32[2,128,512]{2,1,0:T(8,128)S(1)} %get-tuple-element.29.after_any), custom_call_target="tpu_custom_call" | custom-call | flops 6442450944 | bytes 1048576 | tf_op jit(solution)/shard_map/near/pallas_call | solution.py:470
  75.4 1.8 %collective-permute-start.7 = (f32[2,128,512]{2,1,0:T(8,128)S(1)}, f32[2,128,512]{2,1,0:T(8,128)S(1)}, u32[]{:S(2)}, u32[]{:S(2)}) collective-permute-start(f32[2,128,512]{2,1,0:T(8,128)S(1)} %get-tuple-element.28), channel_id=1, source_target_pairs={{0,4},{1,5},{2,6},{3,7},{4,0},{5,1},{6,2},{7,3},{8,12},{9,13},{10,... | collective-permute-start | bytes 1572872 | tf_op jit(solution)/shard_map/ppermute | solution.py:364
  77.2 1.3 %collective-permute-start.12 = (f32[2,128,512]{2,1,0:T(8,128)S(1)}, f32[2,128,512]{2,1,0:T(8,128)S(1)}, u32[]{:S(2)}, u32[]{:S(2)}) collective-permute-start(f32[2,128,512]{2,1,0:T(8,128)S(1)} %add.28), channel_id=1, source_target_pairs={{0,12},{1,13},{2,14},{3,15},{4,8},{5,9},{6,10},{7,11},{8,4},{9,5},... | collective-permute-start | bytes 1572872 | tf_op jit(solution)/shard_map/ppermute | solution.py:364
  78.6 1.2 %collective-permute-start.9 = (f32[2,128,512]{2,1,0:T(8,128)S(1)}, f32[2,128,512]{2,1,0:T(8,128)S(1)}, u32[]{:S(2)}, u32[]{:S(2)}) collective-permute-start(f32[2,128,512]{2,1,0:T(8,128)S(1)} %add.27), channel_id=1, source_target_pairs={{0,4},{1,5},{2,6},{3,7},{4,0},{5,1},{6,2},{7,3},{8,12},{9,13},{10,... | collective-permute-start | bytes 1572872 | tf_op jit(solution)/shard_map/ppermute | solution.py:364
  79.8 1.2 %own.1 = (f32[2,128,512]{2,1,0:T(8,128)S(1)}, f32[2,128,512]{2,1,0:T(8,128)S(1)}) custom-call(bf16[40,2,2,128,256]{4,3,2,1,0:T(8,128)(2,1)S(1)} %get-tuple-element.23.held, bf16[4,1024,512]{2,1,0:T(8,128)(2,1)S(1)} %get-tuple-element.24.right_side), custom_call_target="tpu_custom_call" | custom-call | flops 6442450944 | bytes 1048576 | tf_op jit(solution)/shard_map/own/pallas_call | solution.py:486
  81.0 4.2 %collective-permute-done.10.second_free = f32[2,128,512]{2,1,0:T(8,128)S(1)} collective-permute-done((f32[2,128,512]{2,1,0:T(8,128)S(1)}, f32[2,128,512]{2,1,0:T(8,128)S(1)}, u32[]{:S(2)}, u32[]{:S(2)}) %collective-permute-start.10) | collective-permute-done | bytes 524320 | tf_op jit(solution)/shard_map/ppermute | solution.py:364
  85.2 5.6 %collective-permute-done.12.second_joined = f32[2,128,512]{2,1,0:T(8,128)S(1)} collective-permute-done((f32[2,128,512]{2,1,0:T(8,128)S(1)}, f32[2,128,512]{2,1,0:T(8,128)S(1)}, u32[]{:S(2)}, u32[]{:S(2)}) %collective-permute-start.12) | collective-permute-done | bytes 524320 | tf_op jit(solution)/shard_map/ppermute | solution.py:364
  91.1 1.8 %collective-permute-start.13 = (f32[128,512]{1,0:T(8,128)S(1)}, f32[128,512]{1,0:T(8,128)S(1)}, u32[]{:S(2)}, u32[]{:S(2)}) collective-permute-start(f32[128,512]{1,0:T(8,128)S(1)} %get-tuple-element.34), channel_id=1, source_target_pairs={{0,2},{1,3},{2,0},{3,1},{4,6},{5,7},{6,4},{7,5},{8,10},{9,11},{10,... | collective-permute-start | bytes 786440 | tf_op jit(solution)/shard_map/ppermute | solution.py:364
  93.6 1.6 %collective-permute-start.15 = (f32[128,512]{1,0:T(8,128)S(1)}, f32[128,512]{1,0:T(8,128)S(1)}, u32[]{:S(2)}, u32[]{:S(2)}) collective-permute-start(f32[128,512]{1,0:T(8,128)S(1)} %get-tuple-element.36), channel_id=1, source_target_pairs={{0,3},{1,2},{2,1},{3,0},{4,7},{5,6},{6,5},{7,4},{8,11},{9,10},{10,... | collective-permute-start | bytes 786440 | tf_op jit(solution)/shard_map/ppermute | solution.py:364
  95.2 3.8 %collective-permute-done.13 = f32[128,512]{1,0:T(8,128)S(1)} collective-permute-done((f32[128,512]{1,0:T(8,128)S(1)}, f32[128,512]{1,0:T(8,128)S(1)}, u32[]{:S(2)}, u32[]{:S(2)}) %collective-permute-start.13) | collective-permute-done | bytes 262176 | tf_op jit(solution)/shard_map/ppermute | solution.py:364
  99.1 1.7 %collective-permute-done.14 = f32[128,512]{1,0:T(8,128)S(1)} collective-permute-done((f32[128,512]{1,0:T(8,128)S(1)}, f32[128,512]{1,0:T(8,128)S(1)}, u32[]{:S(2)}, u32[]{:S(2)}) %collective-permute-start.14) | collective-permute-done | bytes 262176 | tf_op jit(solution)/shard_map/ppermute | solution.py:364
  100.8 1.1 %collective-permute-done.15 = f32[128,512]{1,0:T(8,128)S(1)} collective-permute-done((f32[128,512]{1,0:T(8,128)S(1)}, f32[128,512]{1,0:T(8,128)S(1)}, u32[]{:S(2)}, u32[]{:S(2)}) %collective-permute-start.15) | collective-permute-done | bytes 262176 | tf_op jit(solution)/shard_map/ppermute | solution.py:364
  (44 shorter events, 6.1 us)
Async XLA Ops:
  8.1 35.6 %all-to-all-start = ((f32[128,24,128]{2,1,0:T(8,128)}), f32[128,24,128]{2,1,0:T(8,128)S(1)}, u32[]{:S(2)}, u32[]{:S(2)}) async-start(f32[128,24,128]{2,1,0:T(8,128)} %bitcast.35), calls=%async_computation | async-start | bytes 3145728 | tf_op jit(solution)/shard_map/all_to_all | solution.py:435
  19.2 12.2 %copy-start.3 = (s32[128,512,1]{1,2,0:T(1,128)S(1)}, s32[128,512,1]{1,2,0:T(1,128)}, u32[]{:S(2)}) copy-start(s32[128,512,1]{1,2,0:T(1,128)} %param.16) | copy-start | bytes 786436
  19.2 12.2 %copy-start.4 = (s32[128]{0:T(128)S(1)}, s32[128]{0:T(128)}, u32[]{:S(2)}) copy-start(s32[128]{0:T(128)} %count_ref.1) | copy-start | bytes 1540
  19.2 12.3 %copy-start.1 = (s32[128,512]{1,0:T(8,128)S(1)}, s32[128,512]{1,0:T(8,128)}, u32[]{:S(2)}) copy-start(s32[128,512]{1,0:T(8,128)} %slot_ref.1) | copy-start | bytes 786436
  19.3 24.4 %copy-start = (f32[2,128,256]{2,1,0:T(8,128)S(1)}, f32[2,128,256]{2,1,0:T(8,128)}, u32[]{:S(2)}) copy-start(f32[2,128,256]{2,1,0:T(8,128)} %parent_ref.1) | copy-start | bytes 786436
  44.3 10.9 %collective-permute-start.3 = (f32[128,512]{1,0:T(8,128)S(1)}, f32[128,512]{1,0:T(8,128)S(1)}, u32[]{:S(2)}, u32[]{:S(2)}) collective-permute-start(f32[128,512]{1,0:T(8,128)S(1)} %extend.1.own_ref), channel_id=1, source_target_pairs={{0,64},{16,80},{32,96},{48,112},{64,0},{80,16},{96,32},{112,48},{1... | collective-permute-start | bytes 786440 | tf_op jit(solution)/shard_map/ppermute | solution.py:352
  45.2 13.4 %collective-permute-start.2 = (f32[128,512]{1,0:T(8,128)S(1)}, f32[128,512]{1,0:T(8,128)S(1)}, u32[]{:S(2)}, u32[]{:S(2)}) collective-permute-start(f32[128,512]{1,0:T(8,128)S(1)} %extend.1.own_ref), channel_id=1, source_target_pairs={{0,96},{16,112},{32,64},{48,80},{64,32},{80,48},{96,0},{112,16},{1... | collective-permute-start | bytes 786440 | tf_op jit(solution)/shard_map/ppermute | solution.py:352
  47.9 10.8 %collective-permute-start.1 = (f32[128,512]{1,0:T(8,128)S(1)}, f32[128,512]{1,0:T(8,128)S(1)}, u32[]{:S(2)}, u32[]{:S(2)}) collective-permute-start(f32[128,512]{1,0:T(8,128)S(1)} %extend.1.own_ref), channel_id=1, source_target_pairs={{0,32},{16,48},{32,0},{48,16},{64,96},{80,112},{96,64},{112,80},{1... | collective-permute-start | bytes 786440 | tf_op jit(solution)/shard_map/ppermute | solution.py:352
  47.9 11.3 %collective-permute-start = (f32[128,512]{1,0:T(8,128)S(1)}, f32[128,512]{1,0:T(8,128)S(1)}, u32[]{:S(2)}, u32[]{:S(2)}) collective-permute-start(f32[128,512]{1,0:T(8,128)S(1)} %extend.1.own_ref), channel_id=1, source_target_pairs={{0,16},{16,0},{32,48},{48,32},{64,80},{80,64},{96,112},{112,96},{1... | collective-permute-start | bytes 786440 | tf_op jit(solution)/shard_map/ppermute | solution.py:348
  55.2 4.0 %collective-permute-start.6 = (f32[128,512]{1,0:T(8,128)S(1)}, f32[128,512]{1,0:T(8,128)S(1)}, u32[]{:S(2)}, u32[]{:S(2)}) collective-permute-start(f32[128,512]{1,0:T(8,128)S(1)} %collective-permute-done.3.far_ref), channel_id=1, source_target_pairs={{0,16},{16,0},{32,48},{48,32},{64,80},{80,64},{96,112},{112,96},{1... | collective-permute-start | bytes 786440 | tf_op jit(solution)/shard_map/ppermute | solution.py:348
  58.6 1.5 %collective-permute-start.5 = (f32[128,512]{1,0:T(8,128)S(1)}, f32[128,512]{1,0:T(8,128)S(1)}, u32[]{:S(2)}, u32[]{:S(2)}) collective-permute-start(f32[128,512]{1,0:T(8,128)S(1)} %collective-permute-done.2.next_ref), channel_id=1, source_target_pairs={{0,16},{16,0},{32,48},{48,32},{64,80},{80,64},{96,112},{112,96},{1... | collective-permute-start | bytes 786440 | tf_op jit(solution)/shard_map/ppermute | solution.py:348
  58.7 1.9 %collective-permute-start.4 = (f32[128,512]{1,0:T(8,128)S(1)}, f32[128,512]{1,0:T(8,128)S(1)}, u32[]{:S(2)}, u32[]{:S(2)}) collective-permute-start(f32[128,512]{1,0:T(8,128)S(1)} %collective-permute-done.1.near_ref), channel_id=1, source_target_pairs={{0,16},{16,0},{32,48},{48,32},{64,80},{80,64},{96,112},{112,96},{1... | collective-permute-start | bytes 786440 | tf_op jit(solution)/shard_map/ppermute | solution.py:348
  65.8 12.7 %collective-permute-start.8 = (f32[2,128,512]{2,1,0:T(8,128)S(1)}, f32[2,128,512]{2,1,0:T(8,128)S(1)}, u32[]{:S(2)}, u32[]{:S(2)}) collective-permute-start(f32[2,128,512]{2,1,0:T(8,128)S(1)} %get-tuple-element.30), channel_id=1, source_target_pairs={{0,12},{1,13},{2,14},{3,15},{4,8},{5,9},{6,10},{7,11},{8,4},{9,5},... | collective-permute-start | bytes 1572872 | tf_op jit(solution)/shard_map/ppermute | solution.py:364
  66.5 10.6 %collective-permute-start.11 = (f32[2,128,512]{2,1,0:T(8,128)S(1)}, f32[2,128,512]{2,1,0:T(8,128)S(1)}, u32[]{:S(2)}, u32[]{:S(2)}) collective-permute-start(f32[2,128,512]{2,1,0:T(8,128)S(1)} %get-tuple-element.27.after_any), channel_id=1, source_target_pairs={{0,4},{1,5},{2,6},{3,7},{4,0},{5,1},{6,2},{7,3},{8,12},{9,13},{10,... | collective-permute-start | bytes 1572872 | tf_op jit(solution)/shard_map/ppermute | solution.py:364
  74.7 10.5 %collective-permute-start.10 = (f32[2,128,512]{2,1,0:T(8,128)S(1)}, f32[2,128,512]{2,1,0:T(8,128)S(1)}, u32[]{:S(2)}, u32[]{:S(2)}) collective-permute-start(f32[2,128,512]{2,1,0:T(8,128)S(1)} %get-tuple-element.31), channel_id=1, source_target_pairs={{0,12},{1,13},{2,14},{3,15},{4,8},{5,9},{6,10},{7,11},{8,4},{9,5},... | collective-permute-start | bytes 1572872 | tf_op jit(solution)/shard_map/ppermute | solution.py:364
  75.4 9.8 %collective-permute-start.7 = (f32[2,128,512]{2,1,0:T(8,128)S(1)}, f32[2,128,512]{2,1,0:T(8,128)S(1)}, u32[]{:S(2)}, u32[]{:S(2)}) collective-permute-start(f32[2,128,512]{2,1,0:T(8,128)S(1)} %get-tuple-element.28), channel_id=1, source_target_pairs={{0,4},{1,5},{2,6},{3,7},{4,0},{5,1},{6,2},{7,3},{8,12},{9,13},{10,... | collective-permute-start | bytes 1572872 | tf_op jit(solution)/shard_map/ppermute | solution.py:364
  77.2 13.6 %collective-permute-start.12 = (f32[2,128,512]{2,1,0:T(8,128)S(1)}, f32[2,128,512]{2,1,0:T(8,128)S(1)}, u32[]{:S(2)}, u32[]{:S(2)}) collective-permute-start(f32[2,128,512]{2,1,0:T(8,128)S(1)} %add.28), channel_id=1, source_target_pairs={{0,12},{1,13},{2,14},{3,15},{4,8},{5,9},{6,10},{7,11},{8,4},{9,5},... | collective-permute-start | bytes 1572872 | tf_op jit(solution)/shard_map/ppermute | solution.py:364
  78.6 12.2 %collective-permute-start.9 = (f32[2,128,512]{2,1,0:T(8,128)S(1)}, f32[2,128,512]{2,1,0:T(8,128)S(1)}, u32[]{:S(2)}, u32[]{:S(2)}) collective-permute-start(f32[2,128,512]{2,1,0:T(8,128)S(1)} %add.27), channel_id=1, source_target_pairs={{0,4},{1,5},{2,6},{3,7},{4,0},{5,1},{6,2},{7,3},{8,12},{9,13},{10,... | collective-permute-start | bytes 1572872 | tf_op jit(solution)/shard_map/ppermute | solution.py:364
  90.8 11.3 %copy-start.6 = (f32[128]{0:T(128)S(1)}, f32[128]{0:T(128)}, u32[]{:S(2)}) copy-start(f32[128]{0:T(128)} %param.22) | copy-start | bytes 1540
  90.8 11.3 %copy-start.7 = (f32[128]{0:T(128)S(1)}, f32[128]{0:T(128)}, u32[]{:S(2)}) copy-start(f32[128]{0:T(128)} %param.23) | copy-start | bytes 1540
  90.8 11.3 %copy-start.8 = (f32[128]{0:T(128)S(1)}, f32[128]{0:T(128)}, u32[]{:S(2)}) copy-start(f32[128]{0:T(128)} %param.21) | copy-start | bytes 1540
  91.1 8.0 %collective-permute-start.13 = (f32[128,512]{1,0:T(8,128)S(1)}, f32[128,512]{1,0:T(8,128)S(1)}, u32[]{:S(2)}, u32[]{:S(2)}) collective-permute-start(f32[128,512]{1,0:T(8,128)S(1)} %get-tuple-element.34), channel_id=1, source_target_pairs={{0,2},{1,3},{2,0},{3,1},{4,6},{5,7},{6,4},{7,5},{8,10},{9,11},{10,... | collective-permute-start | bytes 786440 | tf_op jit(solution)/shard_map/ppermute | solution.py:364
  92.9 7.9 %collective-permute-start.14 = (f32[128,512]{1,0:T(8,128)S(1)}, f32[128,512]{1,0:T(8,128)S(1)}, u32[]{:S(2)}, u32[]{:S(2)}) collective-permute-start(f32[128,512]{1,0:T(8,128)S(1)} %get-tuple-element.35), channel_id=1, source_target_pairs={{0,1},{1,0},{2,3},{3,2},{4,5},{5,4},{6,7},{7,6},{8,9},{9,8},{10,11... | collective-permute-start | bytes 786440 | tf_op jit(solution)/shard_map/ppermute | solution.py:364
  93.6 8.2 %collective-permute-start.15 = (f32[128,512]{1,0:T(8,128)S(1)}, f32[128,512]{1,0:T(8,128)S(1)}, u32[]{:S(2)}, u32[]{:S(2)}) collective-permute-start(f32[128,512]{1,0:T(8,128)S(1)} %get-tuple-element.36), channel_id=1, source_target_pairs={{0,3},{1,2},{2,1},{3,0},{4,7},{5,6},{6,5},{7,4},{8,11},{9,10},{10,... | collective-permute-start | bytes 786440 | tf_op jit(solution)/shard_map/ppermute | solution.py:364
  (2 other events, 12.0 us)

commit v2 on v1

--- a/solution.py
+++ b/solution.py
@@ -57,55 +57,78 @@
 
 
 def leaf_kernel(
-    count_ref, owner_hbm, source_hbm, inv_hbm, low_hbm, out_ref, owner_ref, source_ref, inv_ref, low_ref, sems
+    count_ref, owner_hbm, source_hbm, inv_hbm, low_hbm, out_hbm, owner_ref, source_ref, inv_ref, low_ref, split_ref, out_ref, sems
 ):
     devices, contrib = owner_hbm.shape[0], owner_ref.shape[1]
     myself = whereabouts()[0]
     pivots, breadth = inv_ref.shape[1], source_ref.shape[2]
     groups = 2 * breadth // LANES
+    half = pivots // 2
+
+    def some(former, latter, *at):
+        return former.at[at], latter.at[at]
+
     copies = [
         pltpu.make_async_copy(former, latter, sems.at[i])
         for i, (former, latter) in enumerate(
             (
-                (source_hbm.at[:, pl.ds(0, pivots)], source_ref.at[:, pl.ds(0, pivots)]),
-                (inv_hbm, inv_ref),
                 (owner_hbm.at[myself], owner_ref),
                 (low_hbm, low_ref),
-                (source_hbm.at[:, pl.ds(pivots, contrib)], source_ref.at[:, pl.ds(pivots, contrib)]),
+                some(source_hbm, source_ref, slice(None), pl.ds(0, half)),
+                some(inv_hbm, inv_ref, slice(None), pl.ds(0, half)),
+                some(source_hbm, source_ref, slice(None), pl.ds(half, half)),
+                some(inv_hbm, inv_ref, slice(None), pl.ds(half, half)),
+                some(source_hbm, source_ref, slice(None), pl.ds(pivots, contrib)),
             )
         )
     ]
-    for at in (2, 0, 1, 3, 4):
-        copies[at].start()
-    copies[2].wait()
+    for copy in copies:
+        copy.start()
+    copies[0].wait()
     names = lax.broadcasted_iota(jnp.int32, (devices, contrib), 0)
     position = lax.broadcasted_iota(jnp.int32, (devices, contrib), 1)
     chosen = jnp.where((names == owner_ref[...]) & (position < count_ref[myself]), 1.0, 0.0)
     rank = running_count(chosen) * chosen
-    pick = jnp.concatenate(
-        [jnp.where(rank == k + 1.0, 1.0, 0.0).astype(BF16) for k in range(CAPACITY)], axis=0
+    copies[1].wait()
+    for part in range(2):
+        split_ref[0, part], split_ref[1, part] = halves(low_ref[part])
+    copies[2].wait()
+    copies[3].wait()
+    upper_source = jnp.concatenate([source_ref[0, :half], source_ref[1, :half]], axis=1)
+    upper = dot(
+        left_parts(inv_ref[0, :half, :half], inv_ref[1, :half, :half]), right_parts(upper_source)
     )
-    copies[0].wait()
+    copies[4].wait()
+    copies[5].wait()
     pivot_source = jnp.concatenate([source_ref[0, :pivots], source_ref[1, :pivots]], axis=1)
-    copies[1].wait()
-    half = pivots // 2
-    upper = dot(
-        left_parts(inv_ref[0, :half, :half], inv_ref[1, :half, :half]), right_parts(pivot_source[:half])
-    )
     lower = dot(left_parts(inv_ref[0, half:], inv_ref[1, half:]), right_parts(pivot_source))
-    pivot_part = jnp.concatenate([upper, lower], axis=0)
-    copies[3].wait()
-    eliminated = dot(left_parts(low_ref[0], low_ref[1]), right_parts(pivot_part))
-    copies[4].wait()
+    pivot_part = right_parts(jnp.concatenate([upper, lower], axis=0))
+    high, low = [split_ref[0, part] for part in range(2)], [split_ref[1, part] for part in range(2)]
+    eliminated = dot(jnp.concatenate(high + high + low, axis=1), pivot_part)
+    copies[6].wait()
     update = jnp.concatenate([source_ref[0, pivots:], source_ref[1, pivots:]], axis=1) - eliminated
     high, low = halves(update)
-    rows = dot(jnp.concatenate([pick, pick], axis=1), jnp.concatenate([high, low], axis=0))
-    for k in range(CAPACITY):
-        for g in range(groups):
-            at = (g % 2) * breadth + g // 2 * LANES
-            out_ref[pl.ds(k * groups + g, devices, stride=CAPACITY * groups), :] = rows[
-                k * devices : (k + 1) * devices, at : at + LANES
-            ]
+    both = jnp.concatenate([high, low], axis=0)
+    share = devices // 2
+    outs = []
+    for i in range(2):
+        some_rank = rank[i * share : (i + 1) * share]
+        pick = jnp.concatenate(
+            [jnp.where(some_rank == k + 1.0, 1.0, 0.0).astype(BF16) for k in range(CAPACITY)], axis=0
+        )
+        rows = dot(jnp.concatenate([pick, pick], axis=1), both)
+        first = i * share * CAPACITY * groups
+        for k in range(CAPACITY):
+            for g in range(groups):
+                at = (g % 2) * breadth + g // 2 * LANES
+                out_ref[pl.ds(first + k * groups + g, share, stride=CAPACITY * groups), :] = rows[
+                    k * share : (k + 1) * share, at : at + LANES
+                ]
+        span = pl.ds(first, share * CAPACITY * groups)
+        outs.append(pltpu.make_async_copy(out_ref.at[span], out_hbm.at[span], sems.at[len(copies) + i]))
+        outs[i].start()
+    for copy in outs:
+        copy.wait()
 
 
 def placing_kernel(owner_ref, slot_ref, token_hbm, out_ref):
@@ -178,33 +201,6 @@
 
 def hop_from(own, index):
     return lax.rem(index - own + RING, RING)
-
-
-def each_copy(units_hbm, held, sems, hops, act):
-    _, _, own_core, own_y, own_z = whereabouts()
-
-    def copy(first, count, sem):
-        act(pltpu.make_async_copy(units_hbm.at[pl.ds(first, count)], held.at[pl.ds(first, count)], sems.at[sem]))
-
-    for hop in hops:
-        for band in range(RING):
-
-            @pl.when((own_core == 0) & (hop_from(own_y, band) == hop))
-            def _(band=band):
-                copy(first_unit(band), RING * (band + 1), band)
-
-        @pl.when(own_core == 1)
-        def _(hop=hop):
-            for band in range(RING):
-                copy(first_unit(band, lax.rem(own_z + hop, RING)), band + 1, hop * RING + band)
-
-
-def start_rows(*args):
-    each_copy(*args, lambda copy: copy.start())
-
-
-def wait_rows(*args):
-    each_copy(*args, lambda copy: copy.wait())
 
 
 def product_by_hop(held, right_ref, total, hop, store):
@@ -253,35 +249,44 @@
             ref[slot] = value
 
 
-def far_kernel(
-    units_hbm, own_ref, other_ref, near_ref, next_ref, far_ref, near2_ref, next2_ref, far2_ref,
-    right_side, first, second, held, sems, total,
-):
-    owned = own_ref.shape[0]
+def kinds_of(value):
+    high, low = halves(value)
+    return high, turned(high, SOURCES), low, turned(low, SOURCES)
+
+
+def load_kernel(units_hbm, own_ref, other_ref, far_ref, filled, held, far_out, sem):
+    copy = pltpu.make_async_copy(units_hbm, held, sem)
+    copy.start()
+    for at, ref in enumerate((own_ref, other_ref, far_ref)):
+        for kind, value in enumerate(kinds_of(ref[...])):
+            filled[kind, at] = value
+    far_out[...] = far_ref[...]
+    copy.wait()
+
+
+def far_kernel(filled, held, near_ref, next_ref, near2_ref, next2_ref, far2_ref, right_side, first, second, total):
+    owned = near_ref.shape[0]
     _, own_x, own_core, _, _ = whereabouts()
-
-    def fill():
-        odd_x = lax.rem(own_x, 2)
-        for hop, ref, ref2 in (
-            (0, own_ref, other_ref), (1 + 2 * odd_x, near_ref, near2_ref), (3 - 2 * odd_x, next_ref, next2_ref), (2, far_ref, far2_ref)
-        ):
-            for core, piece in ((own_core, ref), (1 - own_core, ref2)):
-                at = pl.multiple_of((lax.rem(own_x + hop, RING) * 2 + core) * owned, owned)
-                high, low = halves(piece[...])
-                for kind, value in enumerate((high, turned(high, SOURCES), low, turned(low, SOURCES))):
-                    right_side[kind, pl.ds(at, owned), :] = value
-
+    odd_x = lax.rem(own_x, 2)
     odd, _ = first_axis_odd()
+
+    def rows_of(hop, core):
+        return pl.ds(pl.multiple_of((lax.rem(own_x + hop, RING) * 2 + core) * owned, owned), owned)
+
+    for at, place in enumerate((rows_of(0, own_core), rows_of(0, 1 - own_core), rows_of(2, own_core))):
+        for kind in range(4):
+            right_side[kind, place, :] = filled[kind, at]
+    for hop, ref, core in (
+        (1 + 2 * odd_x, near_ref, own_core), (3 - 2 * odd_x, next_ref, own_core), (1 + 2 * odd_x, near2_ref, 1 - own_core),
+        (3 - 2 * odd_x, next2_ref, 1 - own_core), (2, far2_ref, 1 - own_core),
+    ):
+        for kind, value in enumerate(kinds_of(ref[...])):
+            right_side[kind, rows_of(hop, core), :] = value
 
     def store(hop, other_hop, value):
         store_turned((first, second), lax.rem(other_hop // 2 + odd, 2), lax.rem(other_hop, 2), value)
 
-    start_rows(units_hbm, held, sems, (2,))
-    start_rows(units_hbm, held, sems, (1, 3, 0))
-    fill()
-    wait_rows(units_hbm, held, sems, (2,))
     product_by_hop(held, right_side, total, 2, store)
-    wait_rows(units_hbm, held, sems, (1, 3, 0))
 
 
 def near_kernel(way, held, right_side, after_any, free, joined, total):
@@ -394,17 +399,20 @@
     position = jnp.arange(contrib, dtype=jnp.int32)
     owner = jnp.where(position[None, :] < child_count[:, None], child_owner[:, :, 0], -1)
 
+    outgoing_shape = (devices * CAPACITY * width // LANES, LANES)
     outgoing = pl.pallas_call(
         leaf_kernel,
-        out_shape=jax.ShapeDtypeStruct((devices * CAPACITY * width // LANES, LANES), F32),
+        out_shape=jax.ShapeDtypeStruct(outgoing_shape, F32),
         in_specs=[SMEM] + [ANY] * 4,
-        out_specs=VMEM,
+        out_specs=ANY,
         scratch_shapes=[
             pltpu.VMEM((1, contrib), jnp.int32),
             pltpu.VMEM((2,) + leaf_source.shape[2:], F32),
             pltpu.VMEM(leaf_inv.shape[1:], F32),
             pltpu.VMEM(leaf_low.shape[1:], F32),
-            pltpu.SemaphoreType.DMA((5,)),
+            pltpu.VMEM((2,) + leaf_low.shape[1:], BF16),
+            pltpu.VMEM(outgoing_shape, F32),
+            pltpu.SemaphoreType.DMA((9,)),
         ],
         compiler_params=params(60),
         name="leaf",
@@ -446,6 +454,17 @@
 
     other = swap_cores(assembled)
     hops = [move_x(assembled, way) for way in range(3)]
+    filled, held, hops[2] = pl.pallas_call(
+        load_kernel,
+        out_shape=[
+            jax.ShapeDtypeStruct((4, 3, owned, width), BF16), units_shape, jax.ShapeDtypeStruct((owned, width), F32)
+        ],
+        in_specs=[ANY] + [VMEM] * 3,
+        out_specs=[VMEM] * 3,
+        scratch_shapes=[pltpu.SemaphoreType.DMA],
+        compiler_params=params(40),
+        name="load",
+    )(units, assembled, other, hops[2])
     swapped = [swap_cores(value) for value in hops]
 
     two = jax.ShapeDtypeStruct((2, owned, width), F32)
@@ -453,17 +472,17 @@
     total = pltpu.VMEM((RING * owned, width), F32)
 
     def cost(blocks):
-        return pl.CostEstimate(flops=blocks * 6 * rows * depth * width, bytes_accessed=1 << 20, transcendentals=0)
-
-    right_side, first, second, held = pl.pallas_call(
+        return pl.CostEstimate(flops=blocks * rows * depth * width // 8, bytes_accessed=1 << 18, transcendentals=0)
+
+    right_side, first, second = pl.pallas_call(
         far_kernel,
-        out_shape=[jax.ShapeDtypeStruct((4, depth, width), BF16), two, two, units_shape],
-        in_specs=[ANY] + [VMEM] * 8,
-        out_specs=[VMEM] * 4,
-        scratch_shapes=[pltpu.SemaphoreType.DMA((RING * RING,)), total],
+        out_shape=[jax.ShapeDtypeStruct((4, depth, width), BF16), two, two],
+        in_specs=[VMEM] * 7,
+        out_specs=[VMEM] * 3,
+        scratch_shapes=[total],
         compiler_params=params(33),
         name="far",
-    )(units, assembled, other, *hops, *swapped)
+    )(filled, held, *hops[:2], *swapped)
     got_first, got_second = move_by_core(first, 0, 0), move_by_core(second, 0, 1)
 
     def near(way, after):

time: 103 us -> 102 us (level)
  waiting for transfers between devices: 39.6 us -> 37.1 us
  Pallas kernels: 34.5 us -> 36.7 us
    pallas_call x1 -> x2, Pallas kernels: 8.06 us -> 12 us  [the longest x1 7.96 us: per_device(): pl.pallas_call(leaf_kernel, out_shape=jax.ShapeDtypeStruct(outgoing_shape...]
    ppermute x3, waiting for transfers between devices: 10.8 us -> 7.08 us  [move_x(): lax.ppermute(value, 'row', [(i, 2 * partner(i // 2, way) + i % 2) for i i...]
    pallas_call x1, Pallas kernels: 5.27 us -> 3.59 us  [per_device(): pl.pallas_call(far_kernel, out_shape=[jax.ShapeDtypeStruct((4, depth, wid...]
    ppermute x9, starting transfers between devices: 11.4 us -> 10.3 us  [move_by_core(): return lax.ppermute(value, ('row', 'col'), pairs)]
    ppermute x9, waiting for transfers between devices: 16.4 us -> 17.5 us  [move_by_core(): return lax.ppermute(value, ('row', 'col'), pairs)]
  transfers between devices with their start and end apart: 17 -> 17, of which waited for: 10 -> 14; matrix products, arithmetic and copies ran while one was open for 0% -> 0% of each run, Pallas kernels for 20% -> 24%
where the time goes in v2:
time: 102 us
  waiting for transfers between devices  37.1 us (36%)
  Pallas kernels  36.7 us (36%)
  starting transfers between devices  26.3 us (26%)
  other arithmetic  1.08 us (1%)
    ppermute x9, waiting for transfers between devices, move_by_core(): return lax.ppermute(value, ('row', 'col'), pairs)  17.5 us
    pallas_call x1, Pallas kernels, per_device(): pl.pallas_call(split_kernel, out_shape=[units_shape, jax.ShapeDtypeStruct...  12.2 us
    all_to_all x1, starting transfers between devices, per_device(): lax.all_to_all(outgoing.reshape(devices, -1, LANES), ('row', 'col'), spli...  11.2 us
    all_to_all x1, waiting for transfers between devices, per_device(): lax.all_to_all(outgoing.reshape(devices, -1, LANES), ('row', 'col'), spli...  11 us
    ppermute x9, starting transfers between devices, move_by_core(): return lax.ppermute(value, ('row', 'col'), pairs)  10.3 us
    pallas_call x1, Pallas kernels, per_device(): pl.pallas_call(leaf_kernel, out_shape=jax.ShapeDtypeStruct(outgoing_shape...  7.96 us
    ppermute x3, waiting for transfers between devices, move_x(): lax.ppermute(value, 'row', [(i, 2 * partner(i // 2, way) + i % 2) for i i...  7.08 us
    pallas_call x2, Pallas kernels, near(): pl.pallas_call(functools.partial(near_kernel, way), out_shape=[two] * 2,...  6.48 us
  transfers between devices with their start and end apart: 17, of which 14 were waited for; matrix products, arithmetic and copies ran while one was open for 0% of the time, Pallas kernels for 24%

profile of v2, /device:TPU:0, one launch (start us, length us, event | category | flops | bytes accessed | tf_op | source)
XLA Modules:
  0.0 102.1 jit_solution(14884756629717985082)
XLA Ops:
  0.0 8.0 %leaf.1.after_hbm = f32[3072,128]{1,0:T(8,128)} custom-call(s32[128]{0:T(128)} %count_ref.1, s32[128,1,512]{2,1,0:T(1,128)} %bitcast.39, f32[2,1024,256]{2,1,0:T(8,128)} %bitcast.36, f32[2,512,512]{2,1,0:T(8,128)} %bitcast.37, f32[2,512,512]{2,1,0:T(8,128)} %bitcast.38), custom_call_target="tpu_custom_call" | custom-call | tf_op jit(solution)/shard_map/leaf/pallas_call | solution.py:403
  8.0 11.2 %all-to-all-start = ((f32[128,24,128]{2,1,0:T(8,128)}), f32[128,24,128]{2,1,0:T(8,128)S(1)}, u32[]{:S(2)}, u32[]{:S(2)}) async-start(f32[128,24,128]{2,1,0:T(8,128)} %bitcast.35), calls=%async_computation | async-start | bytes 3145728 | tf_op jit(solution)/shard_map/all_to_all | solution.py:443
  19.2 12.2 %split.1 = (bf16[40,2,2,128,256]{4,3,2,1,0:T(8,128)(2,1)}, f32[8,128]{1,0:T(8,128)}) custom-call(f32[2,2048,1024]{2,1,0:T(8,128)} %value_ref.1, f32[3072,128]{1,0:T(8,128)} %leaf.1.after_hbm), custom_call_target="tpu_custom_call" | custom-call | flops 8388608 | bytes 33554432 | tf_op jit(solution)/shard_map/split/pallas_call | solution.py:424
  32.6 11.0 %all-to-all-done = f32[128,24,128]{2,1,0:T(8,128)S(1)} async-done(((f32[128,24,128]{2,1,0:T(8,128)}), f32[128,24,128]{2,1,0:T(8,128)S(1)}, u32[]{:S(2)}, u32[]{:S(2)}) %all-to-all-start) | async-done | bytes 1572896 | tf_op jit(solution)/shard_map/all_to_all | solution.py:443
  44.3 0.9 collective-permute-start.1
  45.2 1.4 %collective-permute-start.2 = (f32[128,512]{1,0:T(8,128)S(1)}, f32[128,512]{1,0:T(8,128)S(1)}, u32[]{:S(2)}, u32[]{:S(2)}) collective-permute-start(f32[128,512]{1,0:T(8,128)S(1)} %extend.1.own_ref), channel_id=1, source_target_pairs={{0,32},{16,48},{32,0},{48,16},{64,96},{80,112},{96,64},{112,80},{1... | collective-permute-start | bytes 786440 | tf_op jit(solution)/shard_map/ppermute | solution.py:357
  46.6 1.8 %collective-permute-start.3 = (f32[128,512]{1,0:T(8,128)S(1)}, f32[128,512]{1,0:T(8,128)S(1)}, u32[]{:S(2)}, u32[]{:S(2)}) collective-permute-start(f32[128,512]{1,0:T(8,128)S(1)} %extend.1.own_ref), channel_id=1, source_target_pairs={{0,96},{16,112},{32,64},{48,80},{64,32},{80,48},{96,0},{112,16},{1... | collective-permute-start | bytes 786440 | tf_op jit(solution)/shard_map/ppermute | solution.py:357
  48.5 6.6 %collective-permute-done.1.far_ref = f32[128,512]{1,0:T(8,128)S(1)} collective-permute-done((f32[128,512]{1,0:T(8,128)S(1)}, f32[128,512]{1,0:T(8,128)S(1)}, u32[]{:S(2)}, u32[]{:S(2)}) %collective-permute-start.1) | collective-permute-done | bytes 262176 | tf_op jit(solution)/shard_map/ppermute | solution.py:357
  55.0 4.0 %load.1 = (bf16[4,3,128,512]{3,2,1,0:T(8,128)(2,1)S(1)}, bf16[40,2,2,128,256]{4,3,2,1,0:T(8,128)(2,1)S(1)}, f32[128,512]{1,0:T(8,128)S(1)}) custom-call(bf16[40,2,2,128,256]{4,3,2,1,0:T(8,128)(2,1)} %get-tuple-element.23.units_hbm, f32[128,512]{1,0:T(8,128)S(1)} %extend.1.own_ref, f32[128,512]{1,0:T(8,128)S(1)} %collective-permute-done.other_ref, ...), custom_call_target="tpu_custom_call" | custom-call | tf_op jit(solution)/shard_map/load/pallas_call | solution.py:457
  61.7 3.6 %far.1 = (bf16[4,1024,512]{2,1,0:T(8,128)(2,1)S(1)}, f32[2,128,512]{2,1,0:T(8,128)S(1)}, f32[2,128,512]{2,1,0:T(8,128)S(1)}) custom-call(bf16[4,3,128,512]{3,2,1,0:T(8,128)(2,1)S(1)} %get-tuple-element.26.filled, bf16[40,2,2,128,256]{4,3,2,1,0:T(8,128)(2,1)S(1)} %get-tuple-element.25.held, f32[128,512]{1,0:T(8,128)S(1)} %collective-permute-done.2.near_ref, ...), custom_call_target="tpu_custom_call" | custom-call | tf_op jit(solution)/shard_map/far/pallas_call | solution.py:477
  65.3 1.7 %collective-permute-start.11 = (f32[2,128,512]{2,1,0:T(8,128)S(1)}, f32[2,128,512]{2,1,0:T(8,128)S(1)}, u32[]{:S(2)}, u32[]{:S(2)}) collective-permute-start(f32[2,128,512]{2,1,0:T(8,128)S(1)} %get-tuple-element.31.after_any), channel_id=1, source_target_pairs={{0,4},{1,5},{2,6},{3,7},{4,0},{5,1},{6,2},{7,3},{8,12},{9,13},{10,... | collective-permute-start | bytes 1572872 | tf_op jit(solution)/shard_map/ppermute | solution.py:369
  67.0 2.3 %near.2 = (f32[2,128,512]{2,1,0:T(8,128)S(1)}, f32[2,128,512]{2,1,0:T(8,128)S(1)}) custom-call(bf16[40,2,2,128,256]{4,3,2,1,0:T(8,128)(2,1)S(1)} %get-tuple-element.25.held, bf16[4,1024,512]{2,1,0:T(8,128)(2,1)S(1)} %get-tuple-element.28.right_side, f32[2,128,512]{2,1,0:T(8,128)S(1)} %get-tuple-element.31.after_any), custom_call_target="tpu_custom_call" | custom-call | flops 134217728 | bytes 262144 | tf_op jit(solution)/shard_map/near/pallas_call | solution.py:489
  69.3 4.1 %near.3 = (f32[2,128,512]{2,1,0:T(8,128)S(1)}, f32[2,128,512]{2,1,0:T(8,128)S(1)}) custom-call(bf16[40,2,2,128,256]{4,3,2,1,0:T(8,128)(2,1)S(1)} %get-tuple-element.25.held, bf16[4,1024,512]{2,1,0:T(8,128)(2,1)S(1)} %get-tuple-element.28.right_side, f32[2,128,512]{2,1,0:T(8,128)S(1)} %get-tuple-element.33.after_any), custom_call_target="tpu_custom_call" | custom-call | flops 134217728 | bytes 262144 | tf_op jit(solution)/shard_map/near/pallas_call | solution.py:489
  73.4 1.4 %collective-permute-start.10 = (f32[2,128,512]{2,1,0:T(8,128)S(1)}, f32[2,128,512]{2,1,0:T(8,128)S(1)}, u32[]{:S(2)}, u32[]{:S(2)}) collective-permute-start(f32[2,128,512]{2,1,0:T(8,128)S(1)} %get-tuple-element.35), channel_id=1, source_target_pairs={{0,12},{1,13},{2,14},{3,15},{4,8},{5,9},{6,10},{7,11},{8,4},{9,5},... | collective-permute-start | bytes 1572872 | tf_op jit(solution)/shard_map/ppermute | solution.py:369
  74.8 1.2 %collective-permute-start.7 = (f32[2,128,512]{2,1,0:T(8,128)S(1)}, f32[2,128,512]{2,1,0:T(8,128)S(1)}, u32[]{:S(2)}, u32[]{:S(2)}) collective-permute-start(f32[2,128,512]{2,1,0:T(8,128)S(1)} %get-tuple-element.32), channel_id=1, source_target_pairs={{0,4},{1,5},{2,6},{3,7},{4,0},{5,1},{6,2},{7,3},{8,12},{9,13},{10,... | collective-permute-start | bytes 1572872 | tf_op jit(solution)/shard_map/ppermute | solution.py:369
  76.1 0.9 collective-permute-start.12
  77.4 1.1 %collective-permute-start.9 = (f32[2,128,512]{2,1,0:T(8,128)S(1)}, f32[2,128,512]{2,1,0:T(8,128)S(1)}, u32[]{:S(2)}, u32[]{:S(2)}) collective-permute-start(f32[2,128,512]{2,1,0:T(8,128)S(1)} %add.27), channel_id=1, source_target_pairs={{0,4},{1,5},{2,6},{3,7},{4,0},{5,1},{6,2},{7,3},{8,12},{9,13},{10,... | collective-permute-start | bytes 1572872 | tf_op jit(solution)/shard_map/ppermute | solution.py:369
  78.5 1.2 %own.1 = (f32[2,128,512]{2,1,0:T(8,128)S(1)}, f32[2,128,512]{2,1,0:T(8,128)S(1)}) custom-call(bf16[40,2,2,128,256]{4,3,2,1,0:T(8,128)(2,1)S(1)} %get-tuple-element.25.held, bf16[4,1024,512]{2,1,0:T(8,128)(2,1)S(1)} %get-tuple-element.28.right_side), custom_call_target="tpu_custom_call" | custom-call | flops 134217728 | bytes 262144 | tf_op jit(solution)/shard_map/own/pallas_call | solution.py:505
  79.7 4.2 %collective-permute-done.10.second_free = f32[2,128,512]{2,1,0:T(8,128)S(1)} collective-permute-done((f32[2,128,512]{2,1,0:T(8,128)S(1)}, f32[2,128,512]{2,1,0:T(8,128)S(1)}, u32[]{:S(2)}, u32[]{:S(2)}) %collective-permute-start.10) | collective-permute-done | bytes 524320 | tf_op jit(solution)/shard_map/ppermute | solution.py:369
  84.0 5.5 %collective-permute-done.12.second_joined = f32[2,128,512]{2,1,0:T(8,128)S(1)} collective-permute-done((f32[2,128,512]{2,1,0:T(8,128)S(1)}, f32[2,128,512]{2,1,0:T(8,128)S(1)}, u32[]{:S(2)}, u32[]{:S(2)}) %collective-permute-start.12) | collective-permute-done | bytes 524320 | tf_op jit(solution)/shard_map/ppermute | solution.py:369
  90.6 1.5 %collective-permute-start.14 = (f32[128,512]{1,0:T(8,128)S(1)}, f32[128,512]{1,0:T(8,128)S(1)}, u32[]{:S(2)}, u32[]{:S(2)}) collective-permute-start(f32[128,512]{1,0:T(8,128)S(1)} %get-tuple-element.39), channel_id=1, source_target_pairs={{0,1},{1,0},{2,3},{3,2},{4,5},{5,4},{6,7},{7,6},{8,9},{9,8},{10,11... | collective-permute-start | bytes 786440 | tf_op jit(solution)/shard_map/ppermute | solution.py:369
  92.0 2.6 %collective-permute-start.15 = (f32[128,512]{1,0:T(8,128)S(1)}, f32[128,512]{1,0:T(8,128)S(1)}, u32[]{:S(2)}, u32[]{:S(2)}) collective-permute-start(f32[128,512]{1,0:T(8,128)S(1)} %get-tuple-element.40), channel_id=1, source_target_pairs={{0,3},{1,2},{2,1},{3,0},{4,7},{5,6},{6,5},{7,4},{8,11},{9,10},{10,... | collective-permute-start | bytes 786440 | tf_op jit(solution)/shard_map/ppermute | solution.py:369
  94.6 3.9 %collective-permute-done.13 = f32[128,512]{1,0:T(8,128)S(1)} collective-permute-done((f32[128,512]{1,0:T(8,128)S(1)}, f32[128,512]{1,0:T(8,128)S(1)}, u32[]{:S(2)}, u32[]{:S(2)}) %collective-permute-start.13) | collective-permute-done | bytes 262176 | tf_op jit(solution)/shard_map/ppermute | solution.py:369
  99.1 2.1 %collective-permute-done.15 = f32[128,512]{1,0:T(8,128)S(1)} collective-permute-done((f32[128,512]{1,0:T(8,128)S(1)}, f32[128,512]{1,0:T(8,128)S(1)}, u32[]{:S(2)}, u32[]{:S(2)}) %collective-permute-start.15) | collective-permute-done | bytes 262176 | tf_op jit(solution)/shard_map/ppermute | solution.py:369
  (45 shorter events, 7.6 us)
Async XLA Ops:
  8.0 35.6 %all-to-all-start = ((f32[128,24,128]{2,1,0:T(8,128)}), f32[128,24,128]{2,1,0:T(8,128)S(1)}, u32[]{:S(2)}, u32[]{:S(2)}) async-start(f32[128,24,128]{2,1,0:T(8,128)} %bitcast.35), calls=%async_computation | async-start | bytes 3145728 | tf_op jit(solution)/shard_map/all_to_all | solution.py:443
  19.1 12.2 %copy-start.3 = (s32[128,512,1]{1,2,0:T(1,128)S(1)}, s32[128,512,1]{1,2,0:T(1,128)}, u32[]{:S(2)}) copy-start(s32[128,512,1]{1,2,0:T(1,128)} %param.16) | copy-start | bytes 786436
  19.1 12.2 %copy-start.4 = (s32[128]{0:T(128)S(1)}, s32[128]{0:T(128)}, u32[]{:S(2)}) copy-start(s32[128]{0:T(128)} %count_ref.1) | copy-start | bytes 1540
  19.2 12.3 %copy-start.1 = (s32[128,512]{1,0:T(8,128)S(1)}, s32[128,512]{1,0:T(8,128)}, u32[]{:S(2)}) copy-start(s32[128,512]{1,0:T(8,128)} %slot_ref.1) | copy-start | bytes 786436
  19.2 24.4 %copy-start = (f32[2,128,256]{2,1,0:T(8,128)S(1)}, f32[2,128,256]{2,1,0:T(8,128)}, u32[]{:S(2)}) copy-start(f32[2,128,256]{2,1,0:T(8,128)} %parent_ref.1) | copy-start | bytes 786436
  44.2 4.3 %collective-permute-start = (f32[128,512]{1,0:T(8,128)S(1)}, f32[128,512]{1,0:T(8,128)S(1)}, u32[]{:S(2)}, u32[]{:S(2)}) collective-permute-start(f32[128,512]{1,0:T(8,128)S(1)} %extend.1.own_ref), channel_id=1, source_target_pairs={{0,16},{16,0},{32,48},{48,32},{64,80},{80,64},{96,112},{112,96},{1... | collective-permute-start | bytes 786440 | tf_op jit(solution)/shard_map/ppermute | solution.py:353
  44.3 10.7 %collective-permute-start.1 = (f32[128,512]{1,0:T(8,128)S(1)}, f32[128,512]{1,0:T(8,128)S(1)}, u32[]{:S(2)}, u32[]{:S(2)}) collective-permute-start(f32[128,512]{1,0:T(8,128)S(1)} %extend.1.own_ref), channel_id=1, source_target_pairs={{0,64},{16,80},{32,96},{48,112},{64,0},{80,16},{96,32},{112,48},{1... | collective-permute-start | bytes 786440 | tf_op jit(solution)/shard_map/ppermute | solution.py:357
  45.2 13.9 %collective-permute-start.2 = (f32[128,512]{1,0:T(8,128)S(1)}, f32[128,512]{1,0:T(8,128)S(1)}, u32[]{:S(2)}, u32[]{:S(2)}) collective-permute-start(f32[128,512]{1,0:T(8,128)S(1)} %extend.1.own_ref), channel_id=1, source_target_pairs={{0,32},{16,48},{32,0},{48,16},{64,96},{80,112},{96,64},{112,80},{1... | collective-permute-start | bytes 786440 | tf_op jit(solution)/shard_map/ppermute | solution.py:357
  46.6 13.5 %collective-permute-start.3 = (f32[128,512]{1,0:T(8,128)S(1)}, f32[128,512]{1,0:T(8,128)S(1)}, u32[]{:S(2)}, u32[]{:S(2)}) collective-permute-start(f32[128,512]{1,0:T(8,128)S(1)} %extend.1.own_ref), channel_id=1, source_target_pairs={{0,96},{16,112},{32,64},{48,80},{64,32},{80,48},{96,0},{112,16},{1... | collective-permute-start | bytes 786440 | tf_op jit(solution)/shard_map/ppermute | solution.py:357
  59.0 1.6 %collective-permute-start.6 = (f32[128,512]{1,0:T(8,128)S(1)}, f32[128,512]{1,0:T(8,128)S(1)}, u32[]{:S(2)}, u32[]{:S(2)}) collective-permute-start(f32[128,512]{1,0:T(8,128)S(1)} %get-tuple-element.27), channel_id=1, source_target_pairs={{0,16},{16,0},{32,48},{48,32},{64,80},{80,64},{96,112},{112,96},{1... | collective-permute-start | bytes 786440 | tf_op jit(solution)/shard_map/ppermute | solution.py:353
  59.1 1.9 %collective-permute-start.4 = (f32[128,512]{1,0:T(8,128)S(1)}, f32[128,512]{1,0:T(8,128)S(1)}, u32[]{:S(2)}, u32[]{:S(2)}) collective-permute-start(f32[128,512]{1,0:T(8,128)S(1)} %collective-permute-done.2.near_ref), channel_id=1, source_target_pairs={{0,16},{16,0},{32,48},{48,32},{64,80},{80,64},{96,112},{112,96},{1... | collective-permute-start | bytes 786440 | tf_op jit(solution)/shard_map/ppermute | solution.py:353
  60.1 1.5 %collective-permute-start.5 = (f32[128,512]{1,0:T(8,128)S(1)}, f32[128,512]{1,0:T(8,128)S(1)}, u32[]{:S(2)}, u32[]{:S(2)}) collective-permute-start(f32[128,512]{1,0:T(8,128)S(1)} %collective-permute-done.3.next_ref), channel_id=1, source_target_pairs={{0,16},{16,0},{32,48},{48,32},{64,80},{80,64},{96,112},{112,96},{1... | collective-permute-start | bytes 786440 | tf_op jit(solution)/shard_map/ppermute | solution.py:353
  65.3 10.7 %collective-permute-start.11 = (f32[2,128,512]{2,1,0:T(8,128)S(1)}, f32[2,128,512]{2,1,0:T(8,128)S(1)}, u32[]{:S(2)}, u32[]{:S(2)}) collective-permute-start(f32[2,128,512]{2,1,0:T(8,128)S(1)} %get-tuple-element.31.after_any), channel_id=1, source_target_pairs={{0,4},{1,5},{2,6},{3,7},{4,0},{5,1},{6,2},{7,3},{8,12},{9,13},{10,... | collective-permute-start | bytes 1572872 | tf_op jit(solution)/shard_map/ppermute | solution.py:369
  67.0 10.4 %collective-permute-start.8 = (f32[2,128,512]{2,1,0:T(8,128)S(1)}, f32[2,128,512]{2,1,0:T(8,128)S(1)}, u32[]{:S(2)}, u32[]{:S(2)}) collective-permute-start(f32[2,128,512]{2,1,0:T(8,128)S(1)} %get-tuple-element.34), channel_id=1, source_target_pairs={{0,12},{1,13},{2,14},{3,15},{4,8},{5,9},{6,10},{7,11},{8,4},{9,5},... | collective-permute-start | bytes 1572872 | tf_op jit(solution)/shard_map/ppermute | solution.py:369
  73.4 10.5 %collective-permute-start.10 = (f32[2,128,512]{2,1,0:T(8,128)S(1)}, f32[2,128,512]{2,1,0:T(8,128)S(1)}, u32[]{:S(2)}, u32[]{:S(2)}) collective-permute-start(f32[2,128,512]{2,1,0:T(8,128)S(1)} %get-tuple-element.35), channel_id=1, source_target_pairs={{0,12},{1,13},{2,14},{3,15},{4,8},{5,9},{6,10},{7,11},{8,4},{9,5},... | collective-permute-start | bytes 1572872 | tf_op jit(solution)/shard_map/ppermute | solution.py:369
  74.8 9.2 %collective-permute-start.7 = (f32[2,128,512]{2,1,0:T(8,128)S(1)}, f32[2,128,512]{2,1,0:T(8,128)S(1)}, u32[]{:S(2)}, u32[]{:S(2)}) collective-permute-start(f32[2,128,512]{2,1,0:T(8,128)S(1)} %get-tuple-element.32), channel_id=1, source_target_pairs={{0,4},{1,5},{2,6},{3,7},{4,0},{5,1},{6,2},{7,3},{8,12},{9,13},{10,... | collective-permute-start | bytes 1572872 | tf_op jit(solution)/shard_map/ppermute | solution.py:369
  76.1 13.5 %collective-permute-start.12 = (f32[2,128,512]{2,1,0:T(8,128)S(1)}, f32[2,128,512]{2,1,0:T(8,128)S(1)}, u32[]{:S(2)}, u32[]{:S(2)}) collective-permute-start(f32[2,128,512]{2,1,0:T(8,128)S(1)} %add.28), channel_id=1, source_target_pairs={{0,12},{1,13},{2,14},{3,15},{4,8},{5,9},{6,10},{7,11},{8,4},{9,5},... | collective-permute-start | bytes 1572872 | tf_op jit(solution)/shard_map/ppermute | solution.py:369
  77.4 12.8 %collective-permute-start.9 = (f32[2,128,512]{2,1,0:T(8,128)S(1)}, f32[2,128,512]{2,1,0:T(8,128)S(1)}, u32[]{:S(2)}, u32[]{:S(2)}) collective-permute-start(f32[2,128,512]{2,1,0:T(8,128)S(1)} %add.27), channel_id=1, source_target_pairs={{0,4},{1,5},{2,6},{3,7},{4,0},{5,1},{6,2},{7,3},{8,12},{9,13},{10,... | collective-permute-start | bytes 1572872 | tf_op jit(solution)/shard_map/ppermute | solution.py:369
  90.2 11.3 %copy-start.6 = (f32[128]{0:T(128)S(1)}, f32[128]{0:T(128)}, u32[]{:S(2)}) copy-start(f32[128]{0:T(128)} %param.22) | copy-start | bytes 1540
  90.2 11.3 %copy-start.7 = (f32[128]{0:T(128)S(1)}, f32[128]{0:T(128)}, u32[]{:S(2)}) copy-start(f32[128]{0:T(128)} %param.23) | copy-start | bytes 1540
  90.2 11.3 %copy-start.8 = (f32[128]{0:T(128)S(1)}, f32[128]{0:T(128)}, u32[]{:S(2)}) copy-start(f32[128]{0:T(128)} %param.21) | copy-start | bytes 1540
  90.5 8.1 %collective-permute-start.13 = (f32[128,512]{1,0:T(8,128)S(1)}, f32[128,512]{1,0:T(8,128)S(1)}, u32[]{:S(2)}, u32[]{:S(2)}) collective-permute-start(f32[128,512]{1,0:T(8,128)S(1)} %get-tuple-element.38), channel_id=1, source_target_pairs={{0,2},{1,3},{2,0},{3,1},{4,6},{5,7},{6,4},{7,5},{8,10},{9,11},{10,... | collective-permute-start | bytes 786440 | tf_op jit(solution)/shard_map/ppermute | solution.py:369
  90.6 8.5 %collective-permute-start.14 = (f32[128,512]{1,0:T(8,128)S(1)}, f32[128,512]{1,0:T(8,128)S(1)}, u32[]{:S(2)}, u32[]{:S(2)}) collective-permute-start(f32[128,512]{1,0:T(8,128)S(1)} %get-tuple-element.39), channel_id=1, source_target_pairs={{0,1},{1,0},{2,3},{3,2},{4,5},{5,4},{6,7},{7,6},{8,9},{9,8},{10,11... | collective-permute-start | bytes 786440 | tf_op jit(solution)/shard_map/ppermute | solution.py:369
  92.0 9.2 %collective-permute-start.15 = (f32[128,512]{1,0:T(8,128)S(1)}, f32[128,512]{1,0:T(8,128)S(1)}, u32[]{:S(2)}, u32[]{:S(2)}) collective-permute-start(f32[128,512]{1,0:T(8,128)S(1)} %get-tuple-element.40), channel_id=1, source_target_pairs={{0,3},{1,2},{2,1},{3,0},{4,7},{5,6},{6,5},{7,4},{8,11},{9,10},{10,... | collective-permute-start | bytes 786440 | tf_op jit(solution)/shard_map/ppermute | solution.py:369
  (2 other events, 12.0 us)

commit v3 on v2

--- a/solution.py
+++ b/solution.py
@@ -326,23 +326,22 @@
                     near[...], after[...] = blocks[1 + 2 * other_turn], blocks[3 - 2 * other_turn]
 
 
-def material_gradient(eliminated, kernel_coef, p_speed, s_speed, density):
-    norming = 1.0 / jnp.sqrt(jnp.float32(SOURCES))
-    fwd_real, fwd_imag, adj_real, adj_imag = (eliminated[:, at * SOURCES : (at + 1) * SOURCES] for at in range(4))
-    k_lambda = jnp.sum(fwd_real * adj_real - fwd_imag * adj_imag, axis=1) * norming
-    k_mu = jnp.sum(fwd_real * adj_imag + fwd_imag * adj_real, axis=1) * norming
-    k_rho = jnp.sum(fwd_real * adj_real + fwd_imag * adj_imag, axis=1) * norming
-    grad_lambda = kernel_coef[0] * k_lambda
-    grad_mu = kernel_coef[1] * k_mu
-    grad_rho = kernel_coef[2] * k_rho
-    first_out = 2.0 * density * p_speed * grad_lambda
-    second_out = 2.0 * density * s_speed * (grad_mu - 2.0 * grad_lambda)
-    third_out = (
-        (p_speed * p_speed - 2.0 * s_speed * s_speed) * grad_lambda
-        + s_speed * s_speed * grad_mu
-        + grad_rho
-    )
-    return jnp.stack([first_out, second_out, third_out])
+def gradient_kernel(keep, far, closest, after, coef, p_speed, s_speed, density, out):
+    norming = SOURCES**-0.5
+    whole = (keep[...] + far[...]) + (closest[...] + after[...])
+    fwd_real, fwd_imag, adj_real, adj_imag = (whole[:, at * SOURCES : (at + 1) * SOURCES] for at in range(4))
+
+    def over_sources(value):
+        return jnp.sum(value.T, axis=0, keepdims=True) * norming
+
+    real, imag = fwd_real * adj_real, fwd_imag * adj_imag
+    grad_lambda = coef[0:1] * over_sources(real - imag)
+    grad_mu = coef[1:2] * over_sources(fwd_real * adj_imag + fwd_imag * adj_real)
+    grad_rho = coef[2:3] * over_sources(real + imag)
+    p, s, rho = p_speed[...], s_speed[...], density[...]
+    out[0:1] = 2.0 * rho * p * grad_lambda
+    out[1:2] = 2.0 * rho * s * (grad_mu - 2.0 * grad_lambda)
+    out[2:3] = (p * p - 2.0 * s * s) * grad_lambda + s * s * grad_mu + grad_rho
 
 
 def partner(at, way):
@@ -520,8 +519,17 @@
         compiler_params=params(16),
         name="settle",
     )(*own, first_free, first_joined, second_free, second_joined)
-    eliminated = keep + move_by_core(far, 1, 2) + move_by_core(closest, 1, 0) + move_by_core(after, 1, 1)
-    return material_gradient(eliminated, kernel_coef, p_speed, s_speed, density)
+    return pl.pallas_call(
+        gradient_kernel,
+        out_shape=jax.ShapeDtypeStruct(kernel_coef.shape, F32),
+        in_specs=[VMEM] * 8,
+        out_specs=VMEM,
+        compiler_params=params(16),
+        name="gradient",
+    )(
+        keep, move_by_core(far, 1, 2), move_by_core(closest, 1, 0), move_by_core(after, 1, 1),
+        kernel_coef, p_speed[None], s_speed[None], density[None],
+    )
 
 
 def solution(mesh):

time: 102 us -> 102 us (level)
  no operation moved by 1% of the time
where the time goes in v3:
time: 102 us
  Pallas kernels  37.4 us (37%)
  waiting for transfers between devices  37.1 us (36%)
  starting transfers between devices  26.3 us (26%)
    ppermute x9, waiting for transfers between devices, move_by_core(): return lax.ppermute(value, ('row', 'col'), pairs)  17.5 us
    pallas_call x1, Pallas kernels, per_device(): pl.pallas_call(split_kernel, out_shape=[units_shape, jax.ShapeDtypeStruct...  12.2 us
    all_to_all x1, starting transfers between devices, per_device(): lax.all_to_all(outgoing.reshape(devices, -1, LANES), ('row', 'col'), spli...  11.2 us
    all_to_all x1, waiting for transfers between devices, per_device(): lax.all_to_all(outgoing.reshape(devices, -1, LANES), ('row', 'col'), spli...  11 us
    ppermute x9, starting transfers between devices, move_by_core(): return lax.ppermute(value, ('row', 'col'), pairs)  10.3 us
    pallas_call x1, Pallas kernels, per_device(): pl.pallas_call(leaf_kernel, out_shape=jax.ShapeDtypeStruct(outgoing_shape...  7.97 us
    ppermute x3, waiting for transfers between devices, move_x(): lax.ppermute(value, 'row', [(i, 2 * partner(i // 2, way) + i % 2) for i i...  7.08 us
    pallas_call x2, Pallas kernels, near(): pl.pallas_call(functools.partial(near_kernel, way), out_shape=[two] * 2,...  6.47 us
  transfers between devices with their start and end apart: 17, of which 14 were waited for; matrix products, arithmetic and copies ran while one was open for 0% of the time, Pallas kernels for 24%

profile of v3, /device:TPU:0, one launch (start us, length us, event | category | flops | bytes accessed | tf_op | source)
XLA Modules:
  0.0 102.0 jit_solution(2021244920027686353)
XLA Ops:
  0.0 8.0 %leaf.1.after_hbm = f32[3072,128]{1,0:T(8,128)} custom-call(s32[128]{0:T(128)} %count_ref.1, s32[128,1,512]{2,1,0:T(1,128)} %bitcast.19, f32[2,1024,256]{2,1,0:T(8,128)} %bitcast.16, f32[2,512,512]{2,1,0:T(8,128)} %bitcast.17, f32[2,512,512]{2,1,0:T(8,128)} %bitcast.18), custom_call_target="tpu_custom_call" | custom-call | tf_op jit(solution)/shard_map/leaf/pallas_call | solution.py:402
  8.0 11.2 %all-to-all-start = ((f32[128,24,128]{2,1,0:T(8,128)}), f32[128,24,128]{2,1,0:T(8,128)S(1)}, u32[]{:S(2)}, u32[]{:S(2)}) async-start(f32[128,24,128]{2,1,0:T(8,128)} %bitcast.15), calls=%async_computation | async-start | bytes 3145728 | tf_op jit(solution)/shard_map/all_to_all | solution.py:442
  19.2 12.2 %split.1 = (bf16[40,2,2,128,256]{4,3,2,1,0:T(8,128)(2,1)}, f32[8,128]{1,0:T(8,128)}) custom-call(f32[2,2048,1024]{2,1,0:T(8,128)} %value_ref.1, f32[3072,128]{1,0:T(8,128)} %leaf.1.after_hbm), custom_call_target="tpu_custom_call" | custom-call | flops 8388608 | bytes 33554432 | tf_op jit(solution)/shard_map/split/pallas_call | solution.py:423
  32.6 11.0 %all-to-all-done = f32[128,24,128]{2,1,0:T(8,128)S(1)} async-done(((f32[128,24,128]{2,1,0:T(8,128)}), f32[128,24,128]{2,1,0:T(8,128)S(1)}, u32[]{:S(2)}, u32[]{:S(2)}) %all-to-all-start) | async-done | bytes 1572896 | tf_op jit(solution)/shard_map/all_to_all | solution.py:442
  44.3 0.9 collective-permute-start.1
  45.2 1.4 %collective-permute-start.2 = (f32[128,512]{1,0:T(8,128)S(1)}, f32[128,512]{1,0:T(8,128)S(1)}, u32[]{:S(2)}, u32[]{:S(2)}) collective-permute-start(f32[128,512]{1,0:T(8,128)S(1)} %extend.1.own_ref), channel_id=1, source_target_pairs={{0,32},{16,48},{32,0},{48,16},{64,96},{80,112},{96,64},{112,80},{1... | collective-permute-start | bytes 786440 | tf_op jit(solution)/shard_map/ppermute | solution.py:356
  46.6 1.8 %collective-permute-start.3 = (f32[128,512]{1,0:T(8,128)S(1)}, f32[128,512]{1,0:T(8,128)S(1)}, u32[]{:S(2)}, u32[]{:S(2)}) collective-permute-start(f32[128,512]{1,0:T(8,128)S(1)} %extend.1.own_ref), channel_id=1, source_target_pairs={{0,96},{16,112},{32,64},{48,80},{64,32},{80,48},{96,0},{112,16},{1... | collective-permute-start | bytes 786440 | tf_op jit(solution)/shard_map/ppermute | solution.py:356
  48.5 6.6 %collective-permute-done.1.far_ref = f32[128,512]{1,0:T(8,128)S(1)} collective-permute-done((f32[128,512]{1,0:T(8,128)S(1)}, f32[128,512]{1,0:T(8,128)S(1)}, u32[]{:S(2)}, u32[]{:S(2)}) %collective-permute-start.1) | collective-permute-done | bytes 262176 | tf_op jit(solution)/shard_map/ppermute | solution.py:356
  55.1 4.0 %load.1 = (bf16[4,3,128,512]{3,2,1,0:T(8,128)(2,1)S(1)}, bf16[40,2,2,128,256]{4,3,2,1,0:T(8,128)(2,1)S(1)}, f32[128,512]{1,0:T(8,128)S(1)}) custom-call(bf16[40,2,2,128,256]{4,3,2,1,0:T(8,128)(2,1)} %get-tuple-element.23.units_hbm, f32[128,512]{1,0:T(8,128)S(1)} %extend.1.own_ref, f32[128,512]{1,0:T(8,128)S(1)} %collective-permute-done.other_ref, ...), custom_call_target="tpu_custom_call" | custom-call | tf_op jit(solution)/shard_map/load/pallas_call | solution.py:456
  61.7 3.6 %far.1 = (bf16[4,1024,512]{2,1,0:T(8,128)(2,1)S(1)}, f32[2,128,512]{2,1,0:T(8,128)S(1)}, f32[2,128,512]{2,1,0:T(8,128)S(1)}) custom-call(bf16[4,3,128,512]{3,2,1,0:T(8,128)(2,1)S(1)} %get-tuple-element.26.filled, bf16[40,2,2,128,256]{4,3,2,1,0:T(8,128)(2,1)S(1)} %get-tuple-element.25.held, f32[128,512]{1,0:T(8,128)S(1)} %collective-permute-done.2.near_ref, ...), custom_call_target="tpu_custom_call" | custom-call | tf_op jit(solution)/shard_map/far/pallas_call | solution.py:476
  65.3 1.7 %collective-permute-start.11 = (f32[2,128,512]{2,1,0:T(8,128)S(1)}, f32[2,128,512]{2,1,0:T(8,128)S(1)}, u32[]{:S(2)}, u32[]{:S(2)}) collective-permute-start(f32[2,128,512]{2,1,0:T(8,128)S(1)} %get-tuple-element.31.after_any), channel_id=1, source_target_pairs={{0,4},{1,5},{2,6},{3,7},{4,0},{5,1},{6,2},{7,3},{8,12},{9,13},{10,... | collective-permute-start | bytes 1572872 | tf_op jit(solution)/shard_map/ppermute | solution.py:368
  67.0 2.3 %near.2 = (f32[2,128,512]{2,1,0:T(8,128)S(1)}, f32[2,128,512]{2,1,0:T(8,128)S(1)}) custom-call(bf16[40,2,2,128,256]{4,3,2,1,0:T(8,128)(2,1)S(1)} %get-tuple-element.25.held, bf16[4,1024,512]{2,1,0:T(8,128)(2,1)S(1)} %get-tuple-element.28.right_side, f32[2,128,512]{2,1,0:T(8,128)S(1)} %get-tuple-element.31.after_any), custom_call_target="tpu_custom_call" | custom-call | flops 134217728 | bytes 262144 | tf_op jit(solution)/shard_map/near/pallas_call | solution.py:488
  69.3 4.1 %near.3 = (f32[2,128,512]{2,1,0:T(8,128)S(1)}, f32[2,128,512]{2,1,0:T(8,128)S(1)}) custom-call(bf16[40,2,2,128,256]{4,3,2,1,0:T(8,128)(2,1)S(1)} %get-tuple-element.25.held, bf16[4,1024,512]{2,1,0:T(8,128)(2,1)S(1)} %get-tuple-element.28.right_side, f32[2,128,512]{2,1,0:T(8,128)S(1)} %get-tuple-element.33.after_any), custom_call_target="tpu_custom_call" | custom-call | flops 134217728 | bytes 262144 | tf_op jit(solution)/shard_map/near/pallas_call | solution.py:488
  73.5 1.4 %collective-permute-start.10 = (f32[2,128,512]{2,1,0:T(8,128)S(1)}, f32[2,128,512]{2,1,0:T(8,128)S(1)}, u32[]{:S(2)}, u32[]{:S(2)}) collective-permute-start(f32[2,128,512]{2,1,0:T(8,128)S(1)} %get-tuple-element.35), channel_id=1, source_target_pairs={{0,12},{1,13},{2,14},{3,15},{4,8},{5,9},{6,10},{7,11},{8,4},{9,5},... | collective-permute-start | bytes 1572872 | tf_op jit(solution)/shard_map/ppermute | solution.py:368
  74.8 1.2 %collective-permute-start.7 = (f32[2,128,512]{2,1,0:T(8,128)S(1)}, f32[2,128,512]{2,1,0:T(8,128)S(1)}, u32[]{:S(2)}, u32[]{:S(2)}) collective-permute-start(f32[2,128,512]{2,1,0:T(8,128)S(1)} %get-tuple-element.32), channel_id=1, source_target_pairs={{0,4},{1,5},{2,6},{3,7},{4,0},{5,1},{6,2},{7,3},{8,12},{9,13},{10,... | collective-permute-start | bytes 1572872 | tf_op jit(solution)/shard_map/ppermute | solution.py:368
  76.1 0.9 collective-permute-start.12
  77.5 1.1 %collective-permute-start.9 = (f32[2,128,512]{2,1,0:T(8,128)S(1)}, f32[2,128,512]{2,1,0:T(8,128)S(1)}, u32[]{:S(2)}, u32[]{:S(2)}) collective-permute-start(f32[2,128,512]{2,1,0:T(8,128)S(1)} %add.6), channel_id=1, source_target_pairs={{0,4},{1,5},{2,6},{3,7},{4,0},{5,1},{6,2},{7,3},{8,12},{9,13},{10,... | collective-permute-start | bytes 1572872 | tf_op jit(solution)/shard_map/ppermute | solution.py:368
  78.5 1.2 %own.1 = (f32[2,128,512]{2,1,0:T(8,128)S(1)}, f32[2,128,512]{2,1,0:T(8,128)S(1)}) custom-call(bf16[40,2,2,128,256]{4,3,2,1,0:T(8,128)(2,1)S(1)} %get-tuple-element.25.held, bf16[4,1024,512]{2,1,0:T(8,128)(2,1)S(1)} %get-tuple-element.28.right_side), custom_call_target="tpu_custom_call" | custom-call | flops 134217728 | bytes 262144 | tf_op jit(solution)/shard_map/own/pallas_call | solution.py:504
  79.8 4.2 %collective-permute-done.10.second_free = f32[2,128,512]{2,1,0:T(8,128)S(1)} collective-permute-done((f32[2,128,512]{2,1,0:T(8,128)S(1)}, f32[2,128,512]{2,1,0:T(8,128)S(1)}, u32[]{:S(2)}, u32[]{:S(2)}) %collective-permute-start.10) | collective-permute-done | bytes 524320 | tf_op jit(solution)/shard_map/ppermute | solution.py:368
  84.0 5.5 %collective-permute-done.12.second_joined = f32[2,128,512]{2,1,0:T(8,128)S(1)} collective-permute-done((f32[2,128,512]{2,1,0:T(8,128)S(1)}, f32[2,128,512]{2,1,0:T(8,128)S(1)}, u32[]{:S(2)}, u32[]{:S(2)}) %collective-permute-start.12) | collective-permute-done | bytes 524320 | tf_op jit(solution)/shard_map/ppermute | solution.py:368
  90.6 1.4 %collective-permute-start.14 = (f32[128,512]{1,0:T(8,128)S(1)}, f32[128,512]{1,0:T(8,128)S(1)}, u32[]{:S(2)}, u32[]{:S(2)}) collective-permute-start(f32[128,512]{1,0:T(8,128)S(1)} %get-tuple-element.39), channel_id=1, source_target_pairs={{0,1},{1,0},{2,3},{3,2},{4,5},{5,4},{6,7},{7,6},{8,9},{9,8},{10,11... | collective-permute-start | bytes 786440 | tf_op jit(solution)/shard_map/ppermute | solution.py:368
  92.0 2.6 %collective-permute-start.15 = (f32[128,512]{1,0:T(8,128)S(1)}, f32[128,512]{1,0:T(8,128)S(1)}, u32[]{:S(2)}, u32[]{:S(2)}) collective-permute-start(f32[128,512]{1,0:T(8,128)S(1)} %get-tuple-element.40), channel_id=1, source_target_pairs={{0,3},{1,2},{2,1},{3,0},{4,7},{5,6},{6,5},{7,4},{8,11},{9,10},{10,... | collective-permute-start | bytes 786440 | tf_op jit(solution)/shard_map/ppermute | solution.py:368
  94.7 3.9 %collective-permute-done.13.far = f32[128,512]{1,0:T(8,128)S(1)} collective-permute-done((f32[128,512]{1,0:T(8,128)S(1)}, f32[128,512]{1,0:T(8,128)S(1)}, u32[]{:S(2)}, u32[]{:S(2)}) %collective-permute-start.13) | collective-permute-done | bytes 262176 | tf_op jit(solution)/shard_map/ppermute | solution.py:368
  99.1 2.2 %collective-permute-done.15.after = f32[128,512]{1,0:T(8,128)S(1)} collective-permute-done((f32[128,512]{1,0:T(8,128)S(1)}, f32[128,512]{1,0:T(8,128)S(1)}, u32[]{:S(2)}, u32[]{:S(2)}) %collective-permute-start.15) | collective-permute-done | bytes 262176 | tf_op jit(solution)/shard_map/ppermute | solution.py:368
  (42 shorter events, 7.5 us)
Async XLA Ops:
  8.0 35.6 %all-to-all-start = ((f32[128,24,128]{2,1,0:T(8,128)}), f32[128,24,128]{2,1,0:T(8,128)S(1)}, u32[]{:S(2)}, u32[]{:S(2)}) async-start(f32[128,24,128]{2,1,0:T(8,128)} %bitcast.15), calls=%async_computation | async-start | bytes 3145728 | tf_op jit(solution)/shard_map/all_to_all | solution.py:442
  19.1 12.2 %copy-start.7 = (s32[128,512,1]{1,2,0:T(1,128)S(1)}, s32[128,512,1]{1,2,0:T(1,128)}, u32[]{:S(2)}) copy-start(s32[128,512,1]{1,2,0:T(1,128)} %param.16) | copy-start | bytes 786436
  19.2 12.3 %copy-start.1 = (s32[128,512]{1,0:T(8,128)S(1)}, s32[128,512]{1,0:T(8,128)}, u32[]{:S(2)}) copy-start(s32[128,512]{1,0:T(8,128)} %slot_ref.1) | copy-start | bytes 786436
  19.2 24.4 %copy-start = (f32[2,128,256]{2,1,0:T(8,128)S(1)}, f32[2,128,256]{2,1,0:T(8,128)}, u32[]{:S(2)}) copy-start(f32[2,128,256]{2,1,0:T(8,128)} %parent_ref.1) | copy-start | bytes 786436
  44.2 4.3 %collective-permute-start = (f32[128,512]{1,0:T(8,128)S(1)}, f32[128,512]{1,0:T(8,128)S(1)}, u32[]{:S(2)}, u32[]{:S(2)}) collective-permute-start(f32[128,512]{1,0:T(8,128)S(1)} %extend.1.own_ref), channel_id=1, source_target_pairs={{0,16},{16,0},{32,48},{48,32},{64,80},{80,64},{96,112},{112,96},{1... | collective-permute-start | bytes 786440 | tf_op jit(solution)/shard_map/ppermute | solution.py:352
  44.3 10.7 %collective-permute-start.1 = (f32[128,512]{1,0:T(8,128)S(1)}, f32[128,512]{1,0:T(8,128)S(1)}, u32[]{:S(2)}, u32[]{:S(2)}) collective-permute-start(f32[128,512]{1,0:T(8,128)S(1)} %extend.1.own_ref), channel_id=1, source_target_pairs={{0,64},{16,80},{32,96},{48,112},{64,0},{80,16},{96,32},{112,48},{1... | collective-permute-start | bytes 786440 | tf_op jit(solution)/shard_map/ppermute | solution.py:356
  45.2 13.9 %collective-permute-start.2 = (f32[128,512]{1,0:T(8,128)S(1)}, f32[128,512]{1,0:T(8,128)S(1)}, u32[]{:S(2)}, u32[]{:S(2)}) collective-permute-start(f32[128,512]{1,0:T(8,128)S(1)} %extend.1.own_ref), channel_id=1, source_target_pairs={{0,32},{16,48},{32,0},{48,16},{64,96},{80,112},{96,64},{112,80},{1... | collective-permute-start | bytes 786440 | tf_op jit(solution)/shard_map/ppermute | solution.py:356
  46.6 13.5 %collective-permute-start.3 = (f32[128,512]{1,0:T(8,128)S(1)}, f32[128,512]{1,0:T(8,128)S(1)}, u32[]{:S(2)}, u32[]{:S(2)}) collective-permute-start(f32[128,512]{1,0:T(8,128)S(1)} %extend.1.own_ref), channel_id=1, source_target_pairs={{0,96},{16,112},{32,64},{48,80},{64,32},{80,48},{96,0},{112,16},{1... | collective-permute-start | bytes 786440 | tf_op jit(solution)/shard_map/ppermute | solution.py:356
  59.1 1.6 %collective-permute-start.6 = (f32[128,512]{1,0:T(8,128)S(1)}, f32[128,512]{1,0:T(8,128)S(1)}, u32[]{:S(2)}, u32[]{:S(2)}) collective-permute-start(f32[128,512]{1,0:T(8,128)S(1)} %get-tuple-element.27), channel_id=1, source_target_pairs={{0,16},{16,0},{32,48},{48,32},{64,80},{80,64},{96,112},{112,96},{1... | collective-permute-start | bytes 786440 | tf_op jit(solution)/shard_map/ppermute | solution.py:352
  59.2 1.9 %collective-permute-start.4 = (f32[128,512]{1,0:T(8,128)S(1)}, f32[128,512]{1,0:T(8,128)S(1)}, u32[]{:S(2)}, u32[]{:S(2)}) collective-permute-start(f32[128,512]{1,0:T(8,128)S(1)} %collective-permute-done.2.near_ref), channel_id=1, source_target_pairs={{0,16},{16,0},{32,48},{48,32},{64,80},{80,64},{96,112},{112,96},{1... | collective-permute-start | bytes 786440 | tf_op jit(solution)/shard_map/ppermute | solution.py:352
  60.2 1.5 %collective-permute-start.5 = (f32[128,512]{1,0:T(8,128)S(1)}, f32[128,512]{1,0:T(8,128)S(1)}, u32[]{:S(2)}, u32[]{:S(2)}) collective-permute-start(f32[128,512]{1,0:T(8,128)S(1)} %collective-permute-done.3.next_ref), channel_id=1, source_target_pairs={{0,16},{16,0},{32,48},{48,32},{64,80},{80,64},{96,112},{112,96},{1... | collective-permute-start | bytes 786440 | tf_op jit(solution)/shard_map/ppermute | solution.py:352
  65.3 10.7 %collective-permute-start.11 = (f32[2,128,512]{2,1,0:T(8,128)S(1)}, f32[2,128,512]{2,1,0:T(8,128)S(1)}, u32[]{:S(2)}, u32[]{:S(2)}) collective-permute-start(f32[2,128,512]{2,1,0:T(8,128)S(1)} %get-tuple-element.31.after_any), channel_id=1, source_target_pairs={{0,4},{1,5},{2,6},{3,7},{4,0},{5,1},{6,2},{7,3},{8,12},{9,13},{10,... | collective-permute-start | bytes 1572872 | tf_op jit(solution)/shard_map/ppermute | solution.py:368
  67.0 10.4 %collective-permute-start.8 = (f32[2,128,512]{2,1,0:T(8,128)S(1)}, f32[2,128,512]{2,1,0:T(8,128)S(1)}, u32[]{:S(2)}, u32[]{:S(2)}) collective-permute-start(f32[2,128,512]{2,1,0:T(8,128)S(1)} %get-tuple-element.34), channel_id=1, source_target_pairs={{0,12},{1,13},{2,14},{3,15},{4,8},{5,9},{6,10},{7,11},{8,4},{9,5},... | collective-permute-start | bytes 1572872 | tf_op jit(solution)/shard_map/ppermute | solution.py:368
  73.5 10.5 %collective-permute-start.10 = (f32[2,128,512]{2,1,0:T(8,128)S(1)}, f32[2,128,512]{2,1,0:T(8,128)S(1)}, u32[]{:S(2)}, u32[]{:S(2)}) collective-permute-start(f32[2,128,512]{2,1,0:T(8,128)S(1)} %get-tuple-element.35), channel_id=1, source_target_pairs={{0,12},{1,13},{2,14},{3,15},{4,8},{5,9},{6,10},{7,11},{8,4},{9,5},... | collective-permute-start | bytes 1572872 | tf_op jit(solution)/shard_map/ppermute | solution.py:368
  74.8 9.2 %collective-permute-start.7 = (f32[2,128,512]{2,1,0:T(8,128)S(1)}, f32[2,128,512]{2,1,0:T(8,128)S(1)}, u32[]{:S(2)}, u32[]{:S(2)}) collective-permute-start(f32[2,128,512]{2,1,0:T(8,128)S(1)} %get-tuple-element.32), channel_id=1, source_target_pairs={{0,4},{1,5},{2,6},{3,7},{4,0},{5,1},{6,2},{7,3},{8,12},{9,13},{10,... | collective-permute-start | bytes 1572872 | tf_op jit(solution)/shard_map/ppermute | solution.py:368
  76.1 13.5 %collective-permute-start.12 = (f32[2,128,512]{2,1,0:T(8,128)S(1)}, f32[2,128,512]{2,1,0:T(8,128)S(1)}, u32[]{:S(2)}, u32[]{:S(2)}) collective-permute-start(f32[2,128,512]{2,1,0:T(8,128)S(1)} %add.7), channel_id=1, source_target_pairs={{0,12},{1,13},{2,14},{3,15},{4,8},{5,9},{6,10},{7,11},{8,4},{9,5},... | collective-permute-start | bytes 1572872 | tf_op jit(solution)/shard_map/ppermute | solution.py:368
  77.5 12.8 %collective-permute-start.9 = (f32[2,128,512]{2,1,0:T(8,128)S(1)}, f32[2,128,512]{2,1,0:T(8,128)S(1)}, u32[]{:S(2)}, u32[]{:S(2)}) collective-permute-start(f32[2,128,512]{2,1,0:T(8,128)S(1)} %add.6), channel_id=1, source_target_pairs={{0,4},{1,5},{2,6},{3,7},{4,0},{5,1},{6,2},{7,3},{8,12},{9,13},{10,... | collective-permute-start | bytes 1572872 | tf_op jit(solution)/shard_map/ppermute | solution.py:368
  79.7 21.5 %copy-start.3 = (f32[3,128]{1,0:T(4,128)S(1)}, f32[3,128]{1,0:T(4,128)}, u32[]{:S(2)}) copy-start(f32[3,128]{1,0:T(4,128)} %coef.1) | copy-start | bytes 4612
  79.8 21.5 %copy-start.4 = (f32[128]{0:T(128)S(1)}, f32[128]{0:T(128)}, u32[]{:S(2)}) copy-start(f32[128]{0:T(128)} %param.21) | copy-start | bytes 1540
  79.8 21.5 %copy-start.5 = (f32[128]{0:T(128)S(1)}, f32[128]{0:T(128)}, u32[]{:S(2)}) copy-start(f32[128]{0:T(128)} %param.22) | copy-start | bytes 1540
  79.8 21.5 %copy-start.6 = (f32[128]{0:T(128)S(1)}, f32[128]{0:T(128)}, u32[]{:S(2)}) copy-start(f32[128]{0:T(128)} %param.23) | copy-start | bytes 1540
  90.5 8.1 %collective-permute-start.13 = (f32[128,512]{1,0:T(8,128)S(1)}, f32[128,512]{1,0:T(8,128)S(1)}, u32[]{:S(2)}, u32[]{:S(2)}) collective-permute-start(f32[128,512]{1,0:T(8,128)S(1)} %get-tuple-element.38), channel_id=1, source_target_pairs={{0,2},{1,3},{2,0},{3,1},{4,6},{5,7},{6,4},{7,5},{8,10},{9,11},{10,... | collective-permute-start | bytes 786440 | tf_op jit(solution)/shard_map/ppermute | solution.py:368
  90.6 8.5 %collective-permute-start.14 = (f32[128,512]{1,0:T(8,128)S(1)}, f32[128,512]{1,0:T(8,128)S(1)}, u32[]{:S(2)}, u32[]{:S(2)}) collective-permute-start(f32[128,512]{1,0:T(8,128)S(1)} %get-tuple-element.39), channel_id=1, source_target_pairs={{0,1},{1,0},{2,3},{3,2},{4,5},{5,4},{6,7},{7,6},{8,9},{9,8},{10,11... | collective-permute-start | bytes 786440 | tf_op jit(solution)/shard_map/ppermute | solution.py:368
  92.0 9.2 %collective-permute-start.15 = (f32[128,512]{1,0:T(8,128)S(1)}, f32[128,512]{1,0:T(8,128)S(1)}, u32[]{:S(2)}, u32[]{:S(2)}) collective-permute-start(f32[128,512]{1,0:T(8,128)S(1)} %get-tuple-element.40), channel_id=1, source_target_pairs={{0,3},{1,2},{2,1},{3,0},{4,7},{5,6},{6,5},{7,4},{8,11},{9,10},{10,... | collective-permute-start | bytes 786440 | tf_op jit(solution)/shard_map/ppermute | solution.py:368
  (2 other events, 12.9 us)
